TPU v7x, 32 devices: a whole 2x2x4 slice. The times are simulated.
32 devices in a mesh: groups: 2 (over x), morton: 16 (over z, y, core).
Axes of the slice: x: 2, y: 2, z: 4, core: 2. Of those that a mesh axis runs over, the one named last changes fastest.
Arguments:
- features: bfloat16 [64, 32, 4096], P(('groups', 'morton')), parts along dimension 0, may hold values from -6 to 6
- voxel_mask: int32 [64, 4096], P(('groups', 'morton')), parts along dimension 0, may hold values 0 or 1
- brick_xy: int32 [64, 2], P('groups'), parts along dimension 0, may hold values from 0 to 3, as said below
- neighbours: int32 [64, 26], P(('groups', 'morton')), parts along dimension 0, may hold values from -1 to 31, as said below
- conv_weight: bfloat16 [32, 864], replicated, may hold values from -0.21875 to 0.21875
- down_weight: bfloat16 [64, 256], replicated, may hold values from -0.375 to 0.375
- coarse_grad: bfloat16 [64, 64, 4096], P(('groups', 'morton')), parts along dimension 0, may hold values from -6 to 6
Outputs:
- coarse_out: bfloat16 [64, 64, 4096], P(('groups', 'morton')), parts along dimension 0
- input_grad: bfloat16 [64, 32, 4096], P(('groups', 'morton')), parts along dimension 0
- conv_grad: float32 [64, 864], P('groups'), parts along dimension 0
- down_grad: float32 [128, 256], P('groups'), parts along dimension 0
There are 2 independent parts, one for each index of `groups`. A program takes and returns all parts, laid end to end along the dimension named above; an argument that names none is the same for every part. Nothing has to cross between parts.
Inputs may be any that keep to these rules, and one draw needn't show every extreme that they name: brick_xy[r] is the (x, y) position of brick r; within a layer no position repeats and the bricks of a layer are in Morton order of (x, y). Brick r lies in z-layer r // 2. neighbours[r, k] is the brick at offset o_k (k < 13) or o_(k+1) (k >= 13) from brick r, with x, y from brick_xy and z the layer, or -1 where that position is empty or outside the 4 x 4 x 32 // 2 grid of positions.
All inputs are finite; a program needn't handle non-finite values. No bound on the sum of `voxel_mask` on one device may be relied on, other than what follows from the above.
Results may differ from a plain program's by a relative error of at most 0.005.
Values may be sent and summed in bfloat16 or wider, within the bound.
No kernel may reach another device: no remote copies, remote signals or barrier semaphores. Data moves between devices by JAX's collectives and lax.ppermute only.
A program may use at most 192 MiB of HBM per device.

v0:
```python
import functools
import math

import jax
import jax.numpy as jnp
from jax import lax
from jax.experimental import pallas as pl
from jax.experimental.pallas import tpu as pltpu
from jax.sharding import PartitionSpec as P

EDGE = 16
HALF = 8
PLANE = EDGE * EDGE
QUARTER = HALF * HALF
BF16 = jnp.bfloat16
F32 = jnp.float32
I32 = jnp.int32
VMEM_LIMIT = 48 * 1024 * 1024


def iota(shape, dim):
    return lax.broadcasted_iota(I32, shape, dim)


def one_hot(row_key, column_key):
    return jnp.where(row_key == column_key, 1.0, 0.0).astype(BF16)


def mm(a, b):
    return jnp.dot(a, b, preferred_element_type=F32)


def mm_nt(a, b):
    return lax.dot_general(a, b, (((1,), (1,)), ((), ())), preferred_element_type=F32)


def xy_of(xy_ref, layer, brick):
    return xy_ref[layer * 2 + brick, 0], xy_ref[layer * 2 + brick, 1]


def octant_key(xy_ref, layer, parity, lane):
    brick = (lane >> 6) & 1
    bases = []
    for b in range(2):
        x, y = xy_of(xy_ref, layer, b)
        base = (x // 2) * PLANE + (y % 2) * HALF * EDGE + (x % 2) * HALF
        bases.append(jnp.where(y // 2 == parity, base, -65536))
    return jnp.where(brick == 0, bases[0], bases[1]) + ((lane >> 3) & 7) * EDGE + (lane & 7)


def first_kernel(layers, xy_ref, grad_ref, feat_ref, mask_ref, low_ref, high_ref, own_ref, send_ref):
    layer = lax.axis_index("morton")
    parity = layer % 2
    for r in range(2):
        for z, ref in ((0, low_ref), (EDGE - 1, high_ref)):
            lanes = pl.ds(z * PLANE, PLANE)
            mask = mask_ref[pl.ds(r, 1), lanes].astype(F32).astype(BF16)
            ref[:, pl.ds(r * PLANE, PLANE)] = feat_ref[r, :, lanes] * mask
    partner = layer + 1 - 2 * parity
    for target, half, ref in ((partner, 1 - parity, send_ref), (layer, parity, own_ref)):
        row = iota((2 * PLANE, 2 * QUARTER), 0)
        lane = iota((2 * PLANE, 2 * QUARTER), 1)
        pick = one_hot(row, octant_key(xy_ref, target, parity, lane))
        for wz in range(HALF):
            lanes = pl.ds(pl.multiple_of((half * HALF + wz) * PLANE, PLANE), PLANE)
            planes = jnp.concatenate([grad_ref[0, :, lanes], grad_ref[1, :, lanes]], axis=1)
            ref[:, pl.ds(wz * 2 * QUARTER, 2 * QUARTER)] = mm(planes, pick).astype(BF16)


def build_selection(xy_ref, layer, other, r, sel_ref):
    x, y = xy_of(xy_ref, layer, r)
    row = iota((2 * PLANE, 128), 0)
    bases = []
    for s in range(2):
        near_x, near_y = xy_of(xy_ref, other, s)
        bases.append((near_y - y) * EDGE * 1024 + (near_x - x) * EDGE)
    row_key = jnp.where(row < PLANE, bases[0], bases[1]) + ((row >> 4) & 15) * 1024 + (row & 15)
    for tile in range(9):
        lane = iota((2 * PLANE, 128), 1) + (tile % 3) * 128
        key = ((lane >> 4) - 1) * 1024 + (lane & 15) + (tile // 3 - 1)
        if tile % 3 == 2:
            key = jnp.where(lane < 18 * EDGE, key, -(1 << 24))
        sel_ref[:, pl.ds(tile * 128, 128)] = one_hot(row_key, key)


def unfold_rows(source, sel_ref, r, first_plane, cols_ref):
    planes = source.shape[0] // 32
    for dx in range(3):
        wide = mm(source, sel_ref[:, dx * 384 : (dx + 1) * 384]).astype(BF16)
        for dy in range(3):
            piece = wide[:, EDGE * dy : EDGE * dy + PLANE]
            for p in range(planes):
                start = (first_plane + p) * 288 + (dy * 3 + dx) * 32
                cols_ref[r, pl.ds(start, 32), :] = piece[p * 32 : (p + 1) * 32]


def unfold_all(xy_ref, layers, own_rows, low, high, sel_ref, cols_ref):
    layer = lax.axis_index("morton")
    for r in range(2):
        build_selection(xy_ref, layer, layer, r, sel_ref)
        for p in range(0, EDGE, 4):
            unfold_rows(own_rows(p, 4), sel_ref, r, 1 + p, cols_ref)
        build_selection(xy_ref, layer, jnp.maximum(layer - 1, 0), r, sel_ref)
        unfold_rows(low, sel_ref, r, 0, cols_ref)
        build_selection(xy_ref, layer, jnp.minimum(layer + 1, layers - 1), r, sel_ref)
        unfold_rows(high, sel_ref, r, EDGE + 1, cols_ref)


def convolve(weight, cols_ref, acc_ref):
    stacked = jnp.concatenate([weight[:, dz * 288 : (dz + 1) * 288] for dz in range(3)], axis=0)
    for r in range(2):
        acc_ref[r] = jnp.zeros(acc_ref.shape[1:], F32)
        for p in range(EDGE + 2):
            rows = pl.ds((EDGE + 1 - p) * 32, 96)
            acc_ref[r, rows, :] += mm(stacked, cols_ref[r, pl.ds(p * 288, 288), :])


def second_kernel(
    layers, scale, xy_ref, feat_ref, mask_ref, low_ref, high_ref, own_ref, recv_ref, weight_ref, down_ref, down_t_ref,
    oct_ref, gplanes_ref, glow_ref, ghigh_ref, sums_ref,
    in_ref, sel_ref, cols_ref, acc_ref, act_ref, up_ref, stride_ref, grad_ref,
):
    for r in range(2):
        for z in range(EDGE):
            lanes = pl.ds(z * PLANE, PLANE)
            mask = mask_ref[pl.ds(r, 1), lanes].astype(F32).astype(BF16)
            in_ref[pl.ds(z * 32, 32), pl.ds(r * PLANE, PLANE)] = feat_ref[r, :, lanes] * mask
    unfold_all(
        xy_ref, layers, lambda p, n: in_ref[pl.ds(p * 32, n * 32), :], low_ref[...], high_ref[...], sel_ref, cols_ref
    )
    convolve(weight_ref[...], cols_ref, acc_ref)

    grad_oct = own_ref[...] + recv_ref[...]
    pieces = jnp.concatenate([grad_oct[:, wz * 128 : (wz + 1) * 128] for wz in range(HALF)], axis=0)
    row = iota((128, PLANE), 0)
    lane = iota((128, PLANE), 1)
    for r in range(2):
        row_key = jnp.where((row >> 6) == r, ((row >> 3) & 7) * 128 + (row & 7) * 2, -65536)
        for k in range(4):
            key = ((lane >> 4) - k // 2) * 64 + (lane & 15) - k % 2
            spread = mm(pieces, one_hot(row_key, key)).astype(BF16)
            for wz in range(HALF):
                up_ref[r, wz, pl.ds(k * 64, 64), :] = spread[wz * 64 : (wz + 1) * 64]
    zeros = jnp.zeros((64, PLANE), BF16)
    for r in range(2):
        grad_ref[r, pl.ds(0, 64), :] = zeros
        grad_ref[r, pl.ds(18 * 32, 64), :] = zeros
        for wz in range(HALF):
            grad_act = mm(down_t_ref[...], up_ref[r, wz])
            for kz in range(2):
                z = 2 * wz + kz
                mask = mask_ref[pl.ds(r, 1), pl.ds(z * PLANE, PLANE)].astype(F32)
                pre = acc_ref[r, pl.ds((17 - z) * 32, 32), :]
                sig = 1.0 / (1.0 + jnp.exp(-pre))
                masked = sig * mask
                act_ref[pl.ds(z * 32, 32), pl.ds(r * PLANE, PLANE)] = (pre * masked).astype(BF16)
                grad = grad_act[kz * 32 : (kz + 1) * 32] * masked * (1.0 + pre * (1.0 - sig))
                grad = grad.astype(BF16)
                grad_ref[r, pl.ds((17 - z) * 32, 32), :] = grad
                gplanes_ref[pl.ds(z * 32, 32), pl.ds(r * PLANE, PLANE)] = grad
                if z == 0:
                    glow_ref[:, pl.ds(r * PLANE, PLANE)] = grad
                if z == EDGE - 1:
                    ghigh_ref[:, pl.ds(r * PLANE, PLANE)] = grad

    row = iota((2 * PLANE, 128), 0)
    lane = iota((2 * PLANE, 128), 1)
    row_key = (row >> 8) * 4096 + ((row >> 4) & 15) * 64 + (row & 15)
    lane_key = (lane >> 6) * 4096 + ((lane >> 3) & 7) * 128 + (lane & 7) * 2
    for k in range(4):
        gather = one_hot(row_key, lane_key + (k // 2) * 64 + k % 2)
        found = mm(act_ref[...], gather).astype(BF16)
        for z in range(EDGE):
            rows = pl.ds((z % 2) * 128 + k * 32, 32)
            stride_ref[rows, pl.ds((z // 2) * 128, 128)] = found[z * 32 : (z + 1) * 32]
    oct_ref[...] = mm(down_ref[...], stride_ref[...]).astype(BF16)
    down_sum = mm_nt(grad_oct, stride_ref[...]) * scale
    sums_ref[:, pl.ds(896, 256)] = down_sum[:32]
    sums_ref[:, pl.ds(1152, 256)] = down_sum[32:]

    total = jnp.zeros((96, 288), F32)
    for r in range(2):
        for p in range(EDGE + 2):
            total += mm_nt(grad_ref[r, pl.ds((EDGE + 1 - p) * 32, 96), :], cols_ref[r, pl.ds(p * 288, 288), :])
    total = total * scale
    sums_ref[:, pl.ds(0, 896)] = jnp.concatenate(
        [total[:32], total[32:64], total[64:], jnp.zeros((32, 32), F32)], axis=1
    )


def third_kernel(
    layers, xy_ref, gplanes_ref, low_ref, high_ref, mask_ref, flipped_ref, out_ref, sel_ref, cols_ref, acc_ref
):
    unfold_all(
        xy_ref, layers, lambda p, n: gplanes_ref[pl.ds(p * 32, n * 32), :], low_ref[...], high_ref[...], sel_ref, cols_ref
    )
    convolve(flipped_ref[...], cols_ref, acc_ref)
    for r in range(2):
        for z in range(EDGE):
            lanes = pl.ds(z * PLANE, PLANE)
            mask = mask_ref[pl.ds(r, 1), lanes].astype(F32)
            out_ref[r, :, lanes] = (acc_ref[r, pl.ds((17 - z) * 32, 32), :] * mask).astype(BF16)


def coarse_kernel(layers, xy_ref, own_ref, recv_ref, out_ref):
    layer = lax.axis_index("morton")
    parity = layer % 2
    partner = layer + 1 - 2 * parity
    for target, half, ref in ((layer, parity, own_ref), (partner, 1 - parity, recv_ref)):
        pieces = jnp.concatenate([ref[:, wz * 128 : (wz + 1) * 128] for wz in range(HALF)], axis=0)
        key = octant_key(xy_ref, target, parity, iota((128, PLANE), 0))
        for q in range(2):
            lane = iota((128, PLANE), 1) + q * PLANE
            placed = mm(pieces, one_hot(key, lane)).astype(BF16)
            for wz in range(HALF):
                lanes = pl.ds(pl.multiple_of((half * HALF + wz) * PLANE, PLANE), PLANE)
                out_ref[q, :, lanes] = placed[wz * 64 : (wz + 1) * 64]


def call(body, name, out_shapes, operands, scratch=(), flops=0, moved=0):
    specs = [pl.BlockSpec(memory_space=pltpu.SMEM)]
    specs += [pl.BlockSpec(memory_space=pltpu.VMEM)] * (len(operands) - 1)
    return pl.pallas_call(
        body,
        name=name,
        out_shape=out_shapes,
        in_specs=specs,
        out_specs=jax.tree.map(lambda _: pl.BlockSpec(memory_space=pltpu.VMEM), out_shapes),
        scratch_shapes=list(scratch),
        compiler_params=pltpu.CompilerParams(vmem_limit_bytes=VMEM_LIMIT),
        cost_estimate=pl.CostEstimate(flops=flops, bytes_accessed=moved, transcendentals=0),
    )(*operands)


def shape(dims, dtype=BF16):
    return jax.ShapeDtypeStruct(dims, dtype)


def exchange(value, bit):
    return lax.ppermute(value, "morton", [(i, i ^ (1 << bit)) for i in range(lax.axis_size("morton"))])


def sum_over_layers(part):
    layers = lax.axis_size("morton")
    rounds = layers.bit_length() - 1
    odd = lax.axis_index("morton") % 2
    rows = part.shape[0] // 2
    keep = lax.dynamic_slice_in_dim(part, odd * rows, rows, 0)
    away = lax.dynamic_slice_in_dim(part, (1 - odd) * rows, rows, 0)
    total = keep + exchange(away, 0)
    for bit in range(1, rounds):
        total = total + exchange(total, bit)
    other = exchange(total, 0)
    return jnp.where(odd == 0, jnp.concatenate([total, other]), jnp.concatenate([other, total]))


def with_both_sides(low_plane, high_plane):
    layers = lax.axis_size("morton")
    up = [(i, i + 1) for i in range(layers - 1)]
    down = [(i + 1, i) for i in range(layers - 1)]
    return lax.ppermute(high_plane, "morton", up), lax.ppermute(low_plane, "morton", down)


def per_device(features, voxel_mask, brick_xy, neighbours, conv_weight, down_weight, coarse_grad):
    bricks, channels, voxels = features.shape
    layers = lax.axis_size("morton")
    scale = 1.0 / math.sqrt(bricks * layers * voxels)
    side_shape = shape((32, 2 * PLANE))
    oct_shape = shape((64, 1024))
    low, high, own, away = call(
        functools.partial(first_kernel, layers), "select", [side_shape, side_shape, oct_shape, oct_shape],
        (brick_xy, coarse_grad, features, voxel_mask), flops=2 * 2**27, moved=2 << 20,
    )
    from_below, from_above = with_both_sides(low, high)
    arrived = exchange(away, 0)
    down_t = down_weight.reshape(64, 2, 4, 32).transpose(1, 3, 2, 0).reshape(64, 256)
    flipped = conv_weight.reshape(32, 27, 32)[:, ::-1, :].transpose(2, 1, 0).reshape(32, 864)
    cols = pltpu.VMEM((2, 18 * 288, PLANE), BF16)
    acc = pltpu.VMEM((2, 20 * 32, PLANE), F32)
    sel = pltpu.VMEM((2 * PLANE, 1152), BF16)
    octants, gplanes, glow, ghigh, sums = call(
        functools.partial(second_kernel, layers, scale), "forward",
        [oct_shape, shape((512, 512)), side_shape, side_shape, shape((32, 1408), F32)],
        (brick_xy, features, voxel_mask, from_below, from_above, own, arrived, conv_weight, down_weight, down_t),
        scratch=[
            pltpu.VMEM((512, 512), BF16), sel, cols, acc, pltpu.VMEM((512, 512), BF16),
            pltpu.VMEM((2, HALF, 256, PLANE), BF16), pltpu.VMEM((256, 1024), BF16), pltpu.VMEM((2, 20 * 32, PLANE), BF16),
        ],
        flops=6 * 2**30, moved=3 << 20,
    )
    grad_below, grad_above = with_both_sides(glow, ghigh)
    octants_there = exchange(octants, 0)
    total = sum_over_layers(sums)
    input_grad = call(
        functools.partial(third_kernel, layers), "backward", shape((bricks, channels, voxels)),
        (brick_xy, gplanes, grad_below, grad_above, voxel_mask, flipped), scratch=[sel, cols, acc],
        flops=3 * 2**30, moved=1 << 20,
    )
    coarse_out = call(
        functools.partial(coarse_kernel, layers), "place", shape((2, 64, voxels)),
        (brick_xy, octants, octants_there), flops=2**28, moved=1 << 20,
    )
    conv_grad = total[:, :864]
    down_grad = jnp.concatenate([total[:, 896:1152], total[:, 1152:]], axis=0)
    return coarse_out, input_grad, conv_grad, down_grad


def solution(mesh):
    return jax.shard_map(
        per_device,
        mesh=mesh,
        in_specs=(
            P(("groups", "morton"), None, None),
            P(("groups", "morton"), None),
            P("groups", None),
            P(("groups", "morton"), None),
            P(),
            P(),
            P(("groups", "morton"), None, None),
        ),
        out_specs=(
            P(("groups", "morton"), None, None),
            P(("groups", "morton"), None, None),
            P("groups", None),
            P("groups", None),
        ),
        check_vma=False,
    )
```

profile of v0, /device:TPU:1, one launch (start us, length us, event | category | flops | bytes accessed | tf_op | source)
XLA Modules:
  0.0 60.5 jit_solution(11828215231939285297)
XLA Ops:
  0.6 0.8 %copy.20.xy_ref = s32[32,2]{1,0:T(8,128)S(1)} copy(s32[32,2]{0,1:T(2,128)} %param.9) | data formatting | bytes 512 | tf_op args[2]
  1.4 0.0 copy-start
  1.4 1.2 %copy-done = bf16[2,64,4096]{2,1,0:T(8,128)(2,1)S(1)} copy-done((bf16[2,64,4096]{2,1,0:T(8,128)(2,1)S(1)}, bf16[2,64,4096]{2,1,0:T(8,128)(2,1)}, u32[]{:S(2)}) %copy-start) | copy-done | bytes 1048600
  2.6 0.0 copy-start.1
  2.6 1.0 %copy-done.1 = bf16[2,32,4096]{2,1,0:T(8,128)(2,1)S(1)} copy-done((bf16[2,32,4096]{2,1,0:T(8,128)(2,1)S(1)}, bf16[2,32,4096]{2,1,0:T(8,128)(2,1)}, u32[]{:S(2)}) %copy-start.1) | copy-done | bytes 524312
  3.7 0.0 copy-start.5
  3.7 0.8 %copy-done.5 = s32[2,4096]{1,0:T(2,128)S(1)} copy-done((s32[2,4096]{1,0:T(2,128)S(1)}, s32[2,4096]{1,0:T(2,128)}, u32[]{:S(2)}) %copy-start.5) | copy-done | bytes 32792
  4.4 0.0 copy-start.2
  4.4 1.3 %select.3 = (bf16[32,512]{1,0:T(8,128)(2,1)S(1)}, bf16[32,512]{1,0:T(8,128)(2,1)S(1)}, bf16[64,1024]{1,0:T(8,128)(2,1)S(1)}, bf16[64,1024]{1,0:T(8,128)(2,1)S(1)}) custom-call(s32[32,2]{1,0:T(8,128)S(1)} %copy.20.xy_ref, bf16[2,64,4096]{2,1,0:T(8,128)(2,1)S(1)} %copy-done, bf16[2,32,4096]{2,1,0:T(8,128)(2,1)S(1)} %copy-done.1, s32[2,4096]{1,0:T(2,128)S(1)} %copy-done.5), custom_call_target="tpu_custom_call" | custom-call | flops 268435456 | bytes 2097152 | tf_op jit(solution)/shard_map/select/pallas_call | solution.py:223
  5.7 0.0 copy-start.4
  5.7 0.1 collective-permute-start.2
  5.8 4.5 %collective-permute-start = (bf16[32,512]{1,0:T(8,128)(2,1)S(1)}, bf16[32,512]{1,0:T(8,128)(2,1)S(1)}, u32[]{:S(2)}, u32[]{:S(2)}) collective-permute-start(bf16[32,512]{1,0:T(8,128)(2,1)S(1)} %get-tuple-element.13), channel_id=1, source_target_pairs={{0,1},{1,2},{2,3},{3,4},{4,5},{5,6},{6,7},{7,8},{8,9},{9,10},{10,1... | collective-permute-start | bytes 98312 | tf_op jit(solution)/shard_map/ppermute | solution.py:261
  10.3 1.9 %collective-permute-start.1 = (bf16[32,512]{1,0:T(8,128)(2,1)S(1)}, bf16[32,512]{1,0:T(8,128)(2,1)S(1)}, u32[]{:S(2)}, u32[]{:S(2)}) collective-permute-start(bf16[32,512]{1,0:T(8,128)(2,1)S(1)} %get-tuple-element.14), channel_id=1, source_target_pairs={{1,0},{2,1},{3,2},{4,3},{5,4},{6,5},{7,6},{8,7},{9,8},{10,9},{11,1... | collective-permute-start | bytes 98312 | tf_op jit(solution)/shard_map/ppermute | solution.py:261
  12.3 0.0 copy-done.4
  12.3 0.1 copy.17
  12.5 0.0 copy-start.3
  12.5 0.0 copy-start.6
  12.5 0.1 reshape.21.down_t_ref
  12.6 0.0 collective-permute-done.low_ref
  12.6 3.0 %collective-permute-done.1.high_ref = bf16[32,512]{1,0:T(8,128)(2,1)S(1)} collective-permute-done((bf16[32,512]{1,0:T(8,128)(2,1)S(1)}, bf16[32,512]{1,0:T(8,128)(2,1)S(1)}, u32[]{:S(2)}, u32[]{:S(2)}) %collective-permute-start.1) | collective-permute-done | bytes 32800 | tf_op jit(solution)/shard_map/ppermute | solution.py:261
  15.6 0.0 collective-permute-done.2.recv_ref
  15.6 0.0 copy-done.2
  15.6 0.0 copy-done.3
  15.6 0.0 copy-done.6
  15.6 11.7 %forward.1 = (bf16[64,1024]{1,0:T(8,128)(2,1)S(1)}, bf16[512,512]{1,0:T(8,128)(2,1)S(1)}, bf16[32,512]{1,0:T(8,128)(2,1)S(1)}, bf16[32,512]{1,0:T(8,128)(2,1)S(1)}, f32[32,1408]{1,0:T(8,128)S(1)}) custom-call(s32[32,2]{1,0:T(8,128)S(1)} %copy.20.xy_ref, bf16[2,32,4096]{2,1,0:T(8,128)(2,1)S(1)} %copy-done.2, s32[2,4096]{1,0:T(2,128)S(1)} %copy-done.6, ...), custom_call_target="tpu_custom_call" | custom-call | flops 6442450944 | bytes 3145728 | tf_op jit(solution)/shard_map/forward/pallas_call | solution.py:223
  27.3 0.1 collective-permute-start.6
  27.4 1.3 %collective-permute-done.6 = f32[16,1408]{1,0:T(8,128)S(1)} collective-permute-done((f32[16,1408]{1,0:T(8,128)S(1)}, f32[16,1408]{1,0:T(8,128)S(1)}, u32[]{:S(2)}, u32[]{:S(2)}) %collective-permute-start.6) | collective-permute-done | bytes 90144 | tf_op jit(solution)/shard_map/ppermute | solution.py:240
  28.7 2.2 %collective-permute-start.7 = (f32[16,1408]{1,0:T(8,128)S(1)}, f32[16,1408]{1,0:T(8,128)S(1)}, u32[]{:S(2)}, u32[]{:S(2)}) collective-permute-start(f32[16,1408]{1,0:T(8,128)S(1)} %dynamic-slice_add_fusion), channel_id=1, source_target_pairs={{0,2},{1,3},{2,0},{3,1},{4,6},{5,7},{6,4},{7,5},{8,10},{9,11},{10,... | collective-permute-start | bytes 270344 | tf_op jit(solution)/shard_map/ppermute | solution.py:240
  30.9 2.8 %collective-permute-done.7 = f32[16,1408]{1,0:T(8,128)S(1)} collective-permute-done((f32[16,1408]{1,0:T(8,128)S(1)}, f32[16,1408]{1,0:T(8,128)S(1)}, u32[]{:S(2)}, u32[]{:S(2)}) %collective-permute-start.7) | collective-permute-done | bytes 90144 | tf_op jit(solution)/shard_map/ppermute | solution.py:240
  33.8 1.4 %collective-permute-start.8 = (f32[16,1408]{1,0:T(8,128)S(1)}, f32[16,1408]{1,0:T(8,128)S(1)}, u32[]{:S(2)}, u32[]{:S(2)}) collective-permute-start(f32[16,1408]{1,0:T(8,128)S(1)} %add.26), channel_id=1, source_target_pairs={{0,4},{1,5},{2,6},{3,7},{4,0},{5,1},{6,2},{7,3},{8,12},{9,13},{10,... | collective-permute-start | bytes 270344 | tf_op jit(solution)/shard_map/ppermute | solution.py:240
  35.1 2.1 %collective-permute-done.8 = f32[16,1408]{1,0:T(8,128)S(1)} collective-permute-done((f32[16,1408]{1,0:T(8,128)S(1)}, f32[16,1408]{1,0:T(8,128)S(1)}, u32[]{:S(2)}, u32[]{:S(2)}) %collective-permute-start.8) | collective-permute-done | bytes 90144 | tf_op jit(solution)/shard_map/ppermute | solution.py:240
  37.2 2.4 %collective-permute-start.9 = (f32[16,1408]{1,0:T(8,128)S(1)}, f32[16,1408]{1,0:T(8,128)S(1)}, u32[]{:S(2)}, u32[]{:S(2)}) collective-permute-start(f32[16,1408]{1,0:T(8,128)S(1)} %add.27), channel_id=1, source_target_pairs={{0,8},{1,9},{2,10},{3,11},{4,12},{5,13},{6,14},{7,15},{8,0},{9,1},... | collective-permute-start | bytes 270344 | tf_op jit(solution)/shard_map/ppermute | solution.py:240
  39.6 5.4 %collective-permute-start.4 = (bf16[32,512]{1,0:T(8,128)(2,1)S(1)}, bf16[32,512]{1,0:T(8,128)(2,1)S(1)}, u32[]{:S(2)}, u32[]{:S(2)}) collective-permute-start(bf16[32,512]{1,0:T(8,128)(2,1)S(1)} %get-tuple-element.19), channel_id=1, source_target_pairs={{0,1},{1,2},{2,3},{3,4},{4,5},{5,6},{6,7},{7,8},{8,9},{9,10},{10,1... | collective-permute-start | bytes 98312 | tf_op jit(solution)/shard_map/ppermute | solution.py:261
  45.0 2.1 %collective-permute-start.5 = (bf16[32,512]{1,0:T(8,128)(2,1)S(1)}, bf16[32,512]{1,0:T(8,128)(2,1)S(1)}, u32[]{:S(2)}, u32[]{:S(2)}) collective-permute-start(bf16[32,512]{1,0:T(8,128)(2,1)S(1)} %get-tuple-element.20), channel_id=1, source_target_pairs={{1,0},{2,1},{3,2},{4,3},{5,4},{6,5},{7,6},{8,7},{9,8},{10,9},{11,1... | collective-permute-start | bytes 98312 | tf_op jit(solution)/shard_map/ppermute | solution.py:261
  47.1 0.2 reshape.22
  47.3 0.2 rev.3
  47.6 0.6 copy.21
  48.1 0.2 reshape.23.flipped_ref
  48.4 0.1 collective-permute-start.3
  48.4 0.0 collective-permute-done.9
  48.5 0.5 collective-permute-start.10
  49.0 0.0 collective-permute-done.4.low_ref
  49.0 1.2 %collective-permute-done.5.high_ref = bf16[32,512]{1,0:T(8,128)(2,1)S(1)} collective-permute-done((bf16[32,512]{1,0:T(8,128)(2,1)S(1)}, bf16[32,512]{1,0:T(8,128)(2,1)S(1)}, u32[]{:S(2)}, u32[]{:S(2)}) %collective-permute-start.5) | collective-permute-done | bytes 32800 | tf_op jit(solution)/shard_map/ppermute | solution.py:261
  50.2 6.7 %backward.1 = bf16[2,32,4096]{2,1,0:T(8,128)(2,1)} custom-call(s32[32,2]{1,0:T(8,128)S(1)} %copy.20.xy_ref, bf16[512,512]{1,0:T(8,128)(2,1)S(1)} %get-tuple-element.18.gplanes_ref, bf16[32,512]{1,0:T(8,128)(2,1)S(1)} %collective-permute-done.4.low_ref, bf16[32,512]{1,0:T(8,128)(2,1)S(1)} %collective-permute-done.5.high_ref, s32[2,4096]{1,0:T(2,128)S(1)} %copy-done.6, ...), custom_call_target="tpu_custom_call" | custom-call | flops 3221225472 | bytes 1048576 | tf_op jit(solution)/shard_map/backward/pallas_call | solution.py:223
  56.9 0.0 collective-permute-done.3.recv_ref
  56.9 2.2 %place.1 = bf16[2,64,4096]{2,1,0:T(8,128)(2,1)} custom-call(s32[32,2]{1,0:T(8,128)S(1)} %copy.20.xy_ref, bf16[64,1024]{1,0:T(8,128)(2,1)S(1)} %get-tuple-element.17.own_ref, bf16[64,1024]{1,0:T(8,128)(2,1)S(1)} %collective-permute-done.3.recv_ref), custom_call_target="tpu_custom_call" | custom-call | flops 268435456 | bytes 1048576 | tf_op jit(solution)/shard_map/place/pallas_call | solution.py:223
  59.1 0.0 collective-permute-done.10
  59.2 0.7 %slice.12 = f32[32,864]{1,0:T(8,128)} slice(f32[32,1408]{1,0:T(8,128)S(1)} %maximum_select_fusion), slice={[0:32], [0:864]} | slice | bytes 221184 | tf_op jit(solution)/shard_map/slice | solution.py:303
  59.8 0.6 %pad_maximum_fusion = f32[64,256]{1,0:T(8,128)} fusion(f32[32,256]{1,0:T(8,128)S(1)} %get-tuple-element.23, f32[32,256]{1,0:T(8,128)S(1)} %get-tuple-element.22), kind=kLoop, calls=%fused_computation.2 | loop fusion | flops 16384 | bytes 131072 | tf_op jit(solution)/shard_map/concatenate | solution.py:304
  (8 shorter events, 0.1 us)
Async XLA Ops:
  1.4 1.2 %copy-start = (bf16[2,64,4096]{2,1,0:T(8,128)(2,1)S(1)}, bf16[2,64,4096]{2,1,0:T(8,128)(2,1)}, u32[]{:S(2)}) copy-start(bf16[2,64,4096]{2,1,0:T(8,128)(2,1)} %grad_ref.1) | copy-start | bytes 3145732
  2.6 1.0 %copy-start.1 = (bf16[2,32,4096]{2,1,0:T(8,128)(2,1)S(1)}, bf16[2,32,4096]{2,1,0:T(8,128)(2,1)}, u32[]{:S(2)}) copy-start(bf16[2,32,4096]{2,1,0:T(8,128)(2,1)} %feat_ref.3) | copy-start | bytes 1572868
  3.7 0.8 %copy-start.5 = (s32[2,4096]{1,0:T(2,128)S(1)}, s32[2,4096]{1,0:T(2,128)}, u32[]{:S(2)}) copy-start(s32[2,4096]{1,0:T(2,128)} %mask_ref.5) | copy-start | bytes 98308
  4.4 11.2 %copy-start.2 = (bf16[2,32,4096]{2,1,0:T(8,128)(2,1)S(1)}, bf16[2,32,4096]{2,1,0:T(8,128)(2,1)}, u32[]{:S(2)}) copy-start(bf16[2,32,4096]{2,1,0:T(8,128)(2,1)} %feat_ref.3) | copy-start | bytes 1572868
  5.7 6.6 %copy-start.4 = (bf16[64,256]{1,0:T(8,128)(2,1)S(1)}, bf16[64,256]{1,0:T(8,128)(2,1)}, u32[]{:S(2)}) copy-start(bf16[64,256]{1,0:T(8,128)(2,1)} %down_ref.1) | copy-start | bytes 98308
  5.7 9.9 %collective-permute-start.2 = (bf16[64,1024]{1,0:T(8,128)(2,1)S(1)}, bf16[64,1024]{1,0:T(8,128)(2,1)S(1)}, u32[]{:S(2)}, u32[]{:S(2)}) collective-permute-start(bf16[64,1024]{1,0:T(8,128)(2,1)S(1)} %get-tuple-element.16), channel_id=1, source_target_pairs={{0,1},{1,0},{2,3},{3,2},{4,5},{5,4},{6,7},{7,6},{8,9},{9,8},{10,11... | collective-permute-start | bytes 393224 | tf_op jit(solution)/shard_map/ppermute | solution.py:240
  5.8 6.8 %collective-permute-start = (bf16[32,512]{1,0:T(8,128)(2,1)S(1)}, bf16[32,512]{1,0:T(8,128)(2,1)S(1)}, u32[]{:S(2)}, u32[]{:S(2)}) collective-permute-start(bf16[32,512]{1,0:T(8,128)(2,1)S(1)} %get-tuple-element.13), channel_id=1, source_target_pairs={{0,1},{1,2},{2,3},{3,4},{4,5},{5,6},{6,7},{7,8},{8,9},{9,10},{10,1... | collective-permute-start | bytes 98312 | tf_op jit(solution)/shard_map/ppermute | solution.py:261
  10.3 5.2 %collective-permute-start.1 = (bf16[32,512]{1,0:T(8,128)(2,1)S(1)}, bf16[32,512]{1,0:T(8,128)(2,1)S(1)}, u32[]{:S(2)}, u32[]{:S(2)}) collective-permute-start(bf16[32,512]{1,0:T(8,128)(2,1)S(1)} %get-tuple-element.14), channel_id=1, source_target_pairs={{1,0},{2,1},{3,2},{4,3},{5,4},{6,5},{7,6},{8,7},{9,8},{10,9},{11,1... | collective-permute-start | bytes 98312 | tf_op jit(solution)/shard_map/ppermute | solution.py:261
  12.5 3.1 %copy-start.3 = (bf16[32,864]{1,0:T(8,128)(2,1)S(1)}, bf16[32,864]{1,0:T(8,128)(2,1)}, u32[]{:S(2)}) copy-start(bf16[32,864]{1,0:T(8,128)(2,1)} %weight_ref.1) | copy-start | bytes 165892
  12.5 3.1 %copy-start.6 = (s32[2,4096]{1,0:T(2,128)S(1)}, s32[2,4096]{1,0:T(2,128)}, u32[]{:S(2)}) copy-start(s32[2,4096]{1,0:T(2,128)} %mask_ref.5) | copy-start | bytes 98308
  27.3 1.4 %collective-permute-start.6 = (f32[16,1408]{1,0:T(8,128)S(1)}, f32[16,1408]{1,0:T(8,128)S(1)}, u32[]{:S(2)}, u32[]{:S(2)}) collective-permute-start(f32[16,1408]{1,0:T(8,128)S(1)} %constant_dynamic-slice_fusion), channel_id=1, source_target_pairs={{0,1},{1,0},{2,3},{3,2},{4,5},{5,4},{6,7},{7,6},{8,9},{9,8},{10,11... | collective-permute-start | bytes 270344 | tf_op jit(solution)/shard_map/ppermute | solution.py:240
  28.7 5.0 %collective-permute-start.7 = (f32[16,1408]{1,0:T(8,128)S(1)}, f32[16,1408]{1,0:T(8,128)S(1)}, u32[]{:S(2)}, u32[]{:S(2)}) collective-permute-start(f32[16,1408]{1,0:T(8,128)S(1)} %dynamic-slice_add_fusion), channel_id=1, source_target_pairs={{0,2},{1,3},{2,0},{3,1},{4,6},{5,7},{6,4},{7,5},{8,10},{9,11},{10,... | collective-permute-start | bytes 270344 | tf_op jit(solution)/shard_map/ppermute | solution.py:240
  33.8 3.4 %collective-permute-start.8 = (f32[16,1408]{1,0:T(8,128)S(1)}, f32[16,1408]{1,0:T(8,128)S(1)}, u32[]{:S(2)}, u32[]{:S(2)}) collective-permute-start(f32[16,1408]{1,0:T(8,128)S(1)} %add.26), channel_id=1, source_target_pairs={{0,4},{1,5},{2,6},{3,7},{4,0},{5,1},{6,2},{7,3},{8,12},{9,13},{10,... | collective-permute-start | bytes 270344 | tf_op jit(solution)/shard_map/ppermute | solution.py:240
  37.2 11.2 %collective-permute-start.9 = (f32[16,1408]{1,0:T(8,128)S(1)}, f32[16,1408]{1,0:T(8,128)S(1)}, u32[]{:S(2)}, u32[]{:S(2)}) collective-permute-start(f32[16,1408]{1,0:T(8,128)S(1)} %add.27), channel_id=1, source_target_pairs={{0,8},{1,9},{2,10},{3,11},{4,12},{5,13},{6,14},{7,15},{8,0},{9,1},... | collective-permute-start | bytes 270344 | tf_op jit(solution)/shard_map/ppermute | solution.py:240
  39.6 9.4 %collective-permute-start.4 = (bf16[32,512]{1,0:T(8,128)(2,1)S(1)}, bf16[32,512]{1,0:T(8,128)(2,1)S(1)}, u32[]{:S(2)}, u32[]{:S(2)}) collective-permute-start(bf16[32,512]{1,0:T(8,128)(2,1)S(1)} %get-tuple-element.19), channel_id=1, source_target_pairs={{0,1},{1,2},{2,3},{3,4},{4,5},{5,6},{6,7},{7,8},{8,9},{9,10},{10,1... | collective-permute-start | bytes 98312 | tf_op jit(solution)/shard_map/ppermute | solution.py:261
  45.0 5.2 %collective-permute-start.5 = (bf16[32,512]{1,0:T(8,128)(2,1)S(1)}, bf16[32,512]{1,0:T(8,128)(2,1)S(1)}, u32[]{:S(2)}, u32[]{:S(2)}) collective-permute-start(bf16[32,512]{1,0:T(8,128)(2,1)S(1)} %get-tuple-element.20), channel_id=1, source_target_pairs={{1,0},{2,1},{3,2},{4,3},{5,4},{6,5},{7,6},{8,7},{9,8},{10,9},{11,1... | collective-permute-start | bytes 98312 | tf_op jit(solution)/shard_map/ppermute | solution.py:261
  48.4 8.5 %collective-permute-start.3 = (bf16[64,1024]{1,0:T(8,128)(2,1)S(1)}, bf16[64,1024]{1,0:T(8,128)(2,1)S(1)}, u32[]{:S(2)}, u32[]{:S(2)}) collective-permute-start(bf16[64,1024]{1,0:T(8,128)(2,1)S(1)} %get-tuple-element.17.own_ref), channel_id=1, source_target_pairs={{0,1},{1,0},{2,3},{3,2},{4,5},{5,4},{6,7},{7,6},{8,9},{9,8},{10,11... | collective-permute-start | bytes 393224 | tf_op jit(solution)/shard_map/ppermute | solution.py:240
  48.5 10.7 %collective-permute-start.10 = (f32[16,1408]{1,0:T(8,128)S(1)}, f32[16,1408]{1,0:T(8,128)S(1)}, u32[]{:S(2)}, u32[]{:S(2)}) collective-permute-start(f32[16,1408]{1,0:T(8,128)S(1)} %add.28), channel_id=1, source_target_pairs={{0,1},{1,0},{2,3},{3,2},{4,5},{5,4},{6,7},{7,6},{8,9},{9,8},{10,11... | collective-permute-start | bytes 270344 | tf_op jit(solution)/shard_map/ppermute | solution.py:240
where the time goes:
time: 60.9 us; the launch traced here: 60.5 us
  Pallas kernels  21.9 us (36%)
  starting transfers between devices  20.7 us (34%)
  waiting for transfers between devices  10.4 us (17%)
  local copies, waits for them, and re-layouts  5.97 us (10%)
  between operations  0.87 us (1%)
  other arithmetic  0.7 us (1%)
    pallas_call x4, Pallas kernels, call(): pl.pallas_call(body, name=name, out_shape=out_shapes, in_specs=specs, out...  21.9 us
    ppermute x2, starting transfers between devices, with_both_sides(): lax.ppermute(high_plane, 'morton', up)  9.89 us
    ppermute x7, starting transfers between devices, exchange(): lax.ppermute(value, 'morton', [(i, i ^ 1 << bit) for i in range(lax.axis_...  6.76 us
    ppermute x7, waiting for transfers between devices, exchange(): lax.ppermute(value, 'morton', [(i, i ^ 1 << bit) for i in range(lax.axis_...  6.2 us
    ppermute x2, waiting for transfers between devices, with_both_sides(): lax.ppermute(low_plane, 'morton', down)  4.18 us
    ppermute x2, starting transfers between devices, with_both_sides(): lax.ppermute(low_plane, 'morton', down)  4.02 us
    unnamed x16, local copies, waits for them, and re-layouts  3.92 us
  transfers between devices with their start and end apart: 11, of which 5 were waited for; matrix products, arithmetic and copies ran while one was open for 2% of the time, Pallas kernels for 15%

commit v1 on v0

v1 whole, which is shorter than its diff:
```python
import functools
import math

import jax
import jax.numpy as jnp
from jax import lax
from jax.experimental import pallas as pl
from jax.experimental.pallas import tpu as pltpu
from jax.sharding import PartitionSpec as P

EDGE = 16
HALF = 8
PLANE = EDGE * EDGE
QUARTER = HALF * HALF
BF16 = jnp.bfloat16
F32 = jnp.float32
I32 = jnp.int32
STEP = 8


def iota(shape, dim):
    return lax.broadcasted_iota(I32, shape, dim)


def one_hot(row_key, column_key):
    return jnp.where(row_key == column_key, 1.0, 0.0).astype(BF16)


def mm(a, b):
    return jnp.dot(a, b, preferred_element_type=F32)


def mm_nt(a, b):
    return lax.dot_general(a, b, (((1,), (1,)), ((), ())), preferred_element_type=F32)


def xy_of(xy_ref, layer, brick):
    return xy_ref[0, layer * 2 + brick], xy_ref[1, layer * 2 + brick]


def octant_key(xy_ref, layer, parity, lane):
    brick = (lane >> 6) & 1
    bases = []
    for b in range(2):
        x, y = xy_of(xy_ref, layer, b)
        base = (x // 2) * PLANE + (y % 2) * HALF * EDGE + (x % 2) * HALF
        bases.append(jnp.where(y // 2 == parity, base, -65536))
    return jnp.where(brick == 0, bases[0], bases[1]) + ((lane >> 3) & 7) * EDGE + (lane & 7)


def start_all(pairs, sems):
    copies = [pltpu.make_async_copy(source, target, sems.at[i]) for i, (source, target) in enumerate(pairs)]
    for copy in copies:
        copy.start()
    return copies


def prepare_kernel(
    xy_ref, feat_hbm, mask_hbm, grad_hbm, weight_hbm, down_hbm,
    core_ref, cross_ref, own_ref, send_ref, flipped_ref, stacked_ref, down_t_ref,
    feat_ref, mask_ref, grad_ref, weight_ref, down_ref, sems,
):
    layer = lax.axis_index("morton")
    parity = layer % 2
    partner = layer + 1 - 2 * parity
    halves = [
        grad_hbm.at[:, :, pl.ds(pl.multiple_of(half * HALF * PLANE, HALF * PLANE), HALF * PLANE)]
        for half in (1 - parity, parity)
    ]
    copies = start_all(
        ((halves[0], grad_ref.at[0]), (halves[1], grad_ref.at[1]), (weight_hbm, weight_ref), (down_hbm, down_ref)), sems
    )
    edges = []
    for side in range(2):
        z = jnp.where(parity == side, EDGE - 1, 0)
        lanes = pl.ds(pl.multiple_of(z * PLANE, PLANE), PLANE)
        edges += start_all(
            ((feat_hbm.at[:, :, lanes], feat_ref.at[side]), (mask_hbm.at[:, lanes], mask_ref.at[side])),
            sems.at[pl.ds(4 + 2 * side, 2)],
        )
    row = iota((2 * PLANE, 2 * QUARTER), 0)
    lane = iota((2 * PLANE, 2 * QUARTER), 1)
    picks = [one_hot(row, octant_key(xy_ref, target, parity, lane)) for target in (partner, layer)]
    for copy in edges:
        copy.wait()
    for side, ref in enumerate((core_ref, cross_ref)):
        for r in range(2):
            mask = mask_ref[side, pl.ds(r, 1), :].astype(F32).astype(BF16)
            ref[:, pl.ds(r * PLANE, PLANE)] = feat_ref[side, r] * mask
    for i, ref in enumerate((send_ref, own_ref)):
        copies[i].wait()
        for wz in range(HALF):
            lanes = pl.ds(wz * PLANE, PLANE)
            planes = jnp.concatenate([grad_ref[i, 0, :, lanes], grad_ref[i, 1, :, lanes]], axis=1)
            ref[:, pl.ds(wz * 2 * QUARTER, 2 * QUARTER)] = mm(planes, picks[i]).astype(BF16)
    copies[2].wait()
    copies[3].wait()
    turned = weight_ref[...].astype(F32).T.astype(BF16)
    for dz in range(3):
        rows = pl.ds(dz * 32, 32)
        blocks = [turned[j * 32 : (j + 1) * 32] for j in (26 - dz * 9 - s for s in range(9))]
        flipped_ref[rows, :] = jnp.concatenate(blocks, axis=1)
        stacked_ref[rows, :] = weight_ref[:, pl.ds(dz * 288, 288)]
    turned = down_ref[...].astype(F32).T.astype(BF16)
    for kz in range(2):
        blocks = [turned[(kz * 4 + k) * 32 : (kz * 4 + k + 1) * 32] for k in range(4)]
        down_t_ref[pl.ds(kz * 32, 32), :] = jnp.concatenate(blocks, axis=1)


def window_mask(shift, ox, oy):
    dy, dx = shift // 3 - 1, shift % 3 - 1
    voxel = (iota((1, PLANE), 1) - (EDGE * dy + dx)) & (PLANE - 1)
    x = (voxel & (EDGE - 1)) + dx - EDGE * ox
    y = (voxel >> 4) + dy - EDGE * oy
    inside = jnp.where(((x | y) & -EDGE) == 0, 1.0, 0.0)
    return jnp.broadcast_to(inside, (32, PLANE)).astype(BF16)


def offset_of(xy_ref, layer, r, other, s):
    x, y = xy_of(xy_ref, layer, r)
    near_x, near_y = xy_of(xy_ref, other, s)
    return near_x - x, near_y - y


def turned(planes, ox):
    return pltpu.roll(planes, (ox * EDGE) & (PLANE - 1), 1)


def shifted(first, second, masks, shift):
    dy, dx = shift // 3 - 1, shift % 3 - 1
    times = first.shape[0] // 32
    both = first * jnp.tile(masks[0], (times, 1)) + second * jnp.tile(masks[1], (times, 1))
    back = (-(EDGE * dy + dx)) & (PLANE - 1)
    return pltpu.roll(both, back, 1) if back else both


def build_masks(xy_ref, layer, r, mask_ref):
    ox, oy = offset_of(xy_ref, layer, r, layer, 1 - r)
    for shift in range(9):
        mask_ref[0, shift] = window_mask(shift, 0, 0)
        mask_ref[1, shift] = window_mask(shift, ox, oy)
    return ox


def unfold_planes(planes_ref, r, ox, mask_ref, cols_ref):
    for p in range(0, EDGE, STEP):
        rows = pl.ds(p * 32, STEP * 32)
        own = planes_ref[rows, pl.ds(r * PLANE, PLANE)]
        other = turned(planes_ref[rows, pl.ds((1 - r) * PLANE, PLANE)], ox)
        for shift in range(9):
            piece = own if shift == 4 else shifted(own, other, (mask_ref[0, shift], mask_ref[1, shift]), shift)
            for q in range(STEP):
                cols_ref[pl.ds((p + q) * 288 + shift * 32, 32), :] = piece[q * 32 : (q + 1) * 32]


def unfold_side(xy_ref, layer, r, other, planes):
    places = [offset_of(xy_ref, layer, r, other, s) for s in range(2)]
    first, second = (turned(planes[:, s * PLANE : (s + 1) * PLANE], places[s][0]) for s in range(2))
    pieces = []
    for shift in range(9):
        masks = [window_mask(shift, ox, oy) for ox, oy in places]
        pieces.append(shifted(first, second, masks, shift))
    return jnp.concatenate(pieces, axis=0)


def convolve(stacked, cols_ref, acc_ref):
    acc_ref[...] = jnp.zeros(acc_ref.shape, F32)
    for p in range(EDGE):
        rows = pl.ds((EDGE - p) * 32, 96)
        acc_ref[rows, :] += mm(stacked, cols_ref[pl.ds(p * 288, 288), :])


def inner_kernel(
    xy_ref, feat_hbm, mask_hbm, stacked_hbm, cols_hbm, acc_hbm,
    feat_ref, mask_ref, stacked_ref, window_ref, in_ref, cols_ref, acc_ref, sems,
):
    layer = lax.axis_index("morton")
    copies = start_all(((feat_hbm, feat_ref), (mask_hbm, mask_ref), (stacked_hbm, stacked_ref)), sems)
    ox = [build_masks(xy_ref, layer, r, window_ref.at[r]) for r in range(2)]
    for copy in copies:
        copy.wait()
    for r in range(2):
        for z in range(EDGE):
            lanes = pl.ds(z * PLANE, PLANE)
            mask = mask_ref[pl.ds(r, 1), lanes].astype(F32).astype(BF16)
            in_ref[pl.ds(z * 32, 32), pl.ds(r * PLANE, PLANE)] = feat_ref[r, :, lanes] * mask
    out = []
    for r in range(2):
        unfold_planes(in_ref, r, ox[r], window_ref.at[r], cols_ref.at[r])
        convolve(stacked_ref[...], cols_ref.at[r], acc_ref.at[r])
        out += start_all(
            ((cols_ref.at[r], cols_hbm.at[r]), (acc_ref.at[r, pl.ds(64, 512)], acc_hbm.at[r, pl.ds(0, 512)])), sems.at[pl.ds(3 + 2 * r, 2)]
        )
    for copy in out:
        copy.wait()


def sides_of(layer, layers):
    odd = layer % 2
    above = layer + 1 - odd
    core = jnp.where(odd == 0, layer + 1, layer - 1)
    cross = jnp.where(odd == 0, jnp.maximum(layer - 1, 0), jnp.minimum(layer + 1, layers - 1))
    return ((core, 2 * (1 - odd), 15 * (1 - odd)), (cross, 2 * odd, 15 * odd))


def rows_at(index):
    return pl.ds(pl.multiple_of(index * 32, 32), 32)


def outer_kernel(
    layers, scale, xy_ref, cols_hbm, acc_hbm, mask_hbm, down_hbm, core_ref, cross_ref, own_ref, recv_ref, stacked_ref, down_t_ref,
    oct_ref, gplanes_ref, gcore_ref, gcross_ref, sums_ref,
    cols_ref, acc_ref, mask_ref, down_ref, act_ref, up_ref, stride_ref, grad_ref, total_ref, sems,
):
    copies = start_all(
        ((acc_hbm.at[:, pl.ds(0, 512)], acc_ref), (mask_hbm, mask_ref), (down_hbm, down_ref), (cols_hbm, cols_ref)), sems
    )
    layer = lax.axis_index("morton")
    sides = sides_of(layer, layers)

    grad_oct = own_ref[...] + recv_ref[...]
    pieces = jnp.concatenate([grad_oct[:, wz * 128 : (wz + 1) * 128] for wz in range(HALF)], axis=0)
    row = iota((128, PLANE), 0)
    lane = iota((128, PLANE), 1)
    parities = []
    for k in range(4):
        voxel = iota((1, PLANE), 1)
        hit = jnp.where(((voxel >> 4) & 1) * 2 + (voxel & 1) == k, 1.0, 0.0)
        parities.append(jnp.broadcast_to(hit, (64, PLANE)).astype(BF16))
    for r in range(2):
        row_key = jnp.where((row >> 6) == r, row & 63, -1)
        spread = mm(pieces, one_hot(row_key, (lane >> 5) * HALF + ((lane >> 1) & 7))).astype(BF16)
        for wz in range(HALF):
            for k in range(4):
                up_ref[r, wz, pl.ds(k * 64, 64), :] = spread[wz * 64 : (wz + 1) * 64] * parities[k]
    side_cols = []
    for (other, dz, z), ref in zip(sides, (core_ref, cross_ref)):
        for r in range(2):
            side_cols.append(unfold_side(xy_ref, layer, r, other, ref[...]))
    for copy in copies[:3]:
        copy.wait()
    for side, (other, dz, z) in enumerate(sides):
        for r in range(2):
            acc_ref[r, rows_at(15 - z), :] += mm(stacked_ref[rows_at(dz), :], side_cols[side * 2 + r])
    zeros = jnp.zeros((64, PLANE), BF16)
    for r in range(2):
        grad_ref[r, pl.ds(0, 64), :] = zeros
        grad_ref[r, pl.ds(18 * 32, 64), :] = zeros
        for wz in range(HALF):
            grad_act = mm(down_t_ref[...], up_ref[r, wz])
            for kz in range(2):
                z = 2 * wz + kz
                mask = mask_ref[pl.ds(r, 1), pl.ds(z * PLANE, PLANE)].astype(F32)
                pre = acc_ref[r, pl.ds((15 - z) * 32, 32), :]
                sig = 1.0 / (1.0 + jnp.exp(-pre))
                masked = sig * mask
                act_ref[pl.ds(z * 32, 32), pl.ds(r * PLANE, PLANE)] = (pre * masked).astype(BF16)
                grad = grad_act[kz * 32 : (kz + 1) * 32] * masked * (1.0 + pre * (1.0 - sig))
                grad = grad.astype(BF16)
                grad_ref[r, pl.ds((17 - z) * 32, 32), :] = grad
                gplanes_ref[pl.ds(z * 32, 32), pl.ds(r * PLANE, PLANE)] = grad
        for (other, dz, z), ref in zip(sides, (gcore_ref, gcross_ref)):
            ref[:, pl.ds(r * PLANE, PLANE)] = grad_ref[r, rows_at(17 - z), :]

    row = iota((2 * PLANE, PLANE), 0)
    lane = iota((2 * PLANE, PLANE), 1)
    row_key = (row >> 8) * 4096 + ((row >> 4) & 15) * 64 + (row & 15)
    lane_key = ((lane >> 6) & 1) * 4096 + ((lane >> 3) & 7) * 128 + (lane & 7) * 2 + (lane >> 7)
    for ky in range(2):
        found = mm(act_ref[...], one_hot(row_key, lane_key + ky * 64)).astype(BF16)
        for z in range(EDGE):
            for kx in range(2):
                rows = pl.ds((z % 2) * 128 + (ky * 2 + kx) * 32, 32)
                stride_ref[rows, pl.ds((z // 2) * 128, 128)] = found[z * 32 : (z + 1) * 32, kx * 128 : (kx + 1) * 128]
    oct_ref[...] = mm(down_ref[...], stride_ref[...]).astype(BF16)
    down_sum = mm_nt(grad_oct, stride_ref[...]) * scale
    sums_ref[:, pl.ds(896, 256)] = down_sum[:32]
    sums_ref[:, pl.ds(1152, 256)] = down_sum[32:]

    copies[3].wait()
    total = jnp.zeros((288, 96), F32)
    for r in range(2):
        for p in range(EDGE):
            total += mm_nt(cols_ref[r, pl.ds(p * 288, 288), :], grad_ref[r, pl.ds((EDGE - p) * 32, 96), :])
    total_ref[...] = total.T
    for side, (other, dz, z) in enumerate(sides):
        for r in range(2):
            total_ref[rows_at(dz), :] += mm_nt(grad_ref[r, rows_at(17 - z), :], side_cols[side * 2 + r])
    total = [total_ref[pl.ds(dz * 32, 32), :] for dz in range(3)]
    sums_ref[:, pl.ds(0, 896)] = jnp.concatenate([*total, jnp.zeros((32, 32), F32)], axis=1) * scale


def back_inner_kernel(r, xy_ref, after_ref, gplanes_ref, flipped_ref, acc_ref, window_ref, cols_ref):
    layer = lax.axis_index("morton")
    ox = build_masks(xy_ref, layer, r, window_ref)
    unfold_planes(gplanes_ref, r, ox, window_ref, cols_ref)
    convolve(flipped_ref[...], cols_ref, acc_ref)


def back_outer_kernel(
    layers, xy_ref, mask_hbm, after_ref, acc0_ref, acc1_ref, core_ref, cross_ref, flipped_ref, out_ref,
    mask_ref, sums_ref, sems,
):
    copies = start_all(((mask_hbm, mask_ref),), sems)
    layer = lax.axis_index("morton")
    sides = sides_of(layer, layers)
    for r, acc_ref in enumerate((acc0_ref, acc1_ref)):
        sums_ref[r] = acc_ref[pl.ds(64, 512), :]
        for (other, dz, z), ref in zip(sides, (core_ref, cross_ref)):
            cols = unfold_side(xy_ref, layer, r, other, ref[...])
            sums_ref[r, rows_at(15 - z), :] += mm(flipped_ref[rows_at(dz), :], cols)
    copies[0].wait()
    for r in range(2):
        for z in range(EDGE):
            lanes = pl.ds(z * PLANE, PLANE)
            mask = mask_ref[pl.ds(r, 1), lanes].astype(F32)
            out_ref[r, :, lanes] = (sums_ref[r, pl.ds((15 - z) * 32, 32), :] * mask).astype(BF16)


def finish_kernel(total_ref, other_ref, conv_ref, down_ref):
    odd = lax.axis_index("morton") % 2
    for place, ref in ((odd, total_ref), (1 - odd, other_ref)):
        rows = pl.ds(pl.multiple_of(place * 16, 16), 16)
        conv_ref[rows, :] = ref[:, pl.ds(0, 864)]
        down_ref[rows, :] = ref[:, pl.ds(896, 256)]
        down_ref[pl.ds(pl.multiple_of(place * 16 + 32, 16), 16), :] = ref[:, pl.ds(1152, 256)]


def coarse_kernel(xy_ref, own_ref, recv_ref, after_ref, out_ref):
    layer = lax.axis_index("morton")
    parity = layer % 2
    partner = layer + 1 - 2 * parity
    for target, half, ref in ((layer, parity, own_ref), (partner, 1 - parity, recv_ref)):
        pieces = jnp.concatenate([ref[:, wz * 128 : (wz + 1) * 128] for wz in range(HALF)], axis=0)
        key = octant_key(xy_ref, target, parity, iota((128, PLANE), 0))
        for q in range(2):
            lane = iota((128, PLANE), 1) + q * PLANE
            placed = mm(pieces, one_hot(key, lane)).astype(BF16)
            for wz in range(HALF):
                lanes = pl.ds(pl.multiple_of((half * HALF + wz) * PLANE, PLANE), PLANE)
                out_ref[q, :, lanes] = placed[wz * 64 : (wz + 1) * 64]


def call(body, name, out_shapes, operands, kinds, scratch=(), us=1, out_kinds=None, vmem_mib=24):
    specs = {"s": pl.BlockSpec(memory_space=pltpu.SMEM), "h": pl.BlockSpec(memory_space=pl.ANY)}
    specs["v"] = pl.BlockSpec(memory_space=pltpu.VMEM)
    single = not isinstance(out_shapes, list)
    out_specs = [specs[kind] for kind in out_kinds or "v" * (1 if single else len(out_shapes))]
    return pl.pallas_call(
        body,
        name=name,
        out_shape=out_shapes,
        in_specs=[specs[kind] for kind in kinds],
        out_specs=out_specs[0] if single else out_specs,
        scratch_shapes=list(scratch),
        compiler_params=pltpu.CompilerParams(vmem_limit_bytes=vmem_mib << 20),
        cost_estimate=pl.CostEstimate(flops=us * 10**9, bytes_accessed=us * 3500000, transcendentals=0),
    )(*operands)


def shape(dims, dtype=BF16):
    return jax.ShapeDtypeStruct(dims, dtype)


def exchange(value, bit):
    return lax.ppermute(value, "morton", [(i, i ^ (1 << bit)) for i in range(lax.axis_size("morton"))])


def exchange_cross(value):
    layers = lax.axis_size("morton")
    pairs = [(i, i + 1) for i in range(1, layers - 1, 2)]
    return lax.ppermute(value, "morton", pairs + [(target, source) for source, target in pairs])


def per_device(features, voxel_mask, brick_xy, neighbours, conv_weight, down_weight, coarse_grad):
    bricks, channels, voxels = features.shape
    layers = lax.axis_size("morton")
    rounds = layers.bit_length() - 1
    scale = 1.0 / math.sqrt(bricks * layers * voxels)
    side_shape = shape((32, 2 * PLANE))
    oct_shape = shape((64, 1024))
    xy = brick_xy.T
    block = shape((96, 288))
    core_edge, cross_edge, own, away, flipped, stacked, down_t = call(
        prepare_kernel, "prepare", [side_shape, side_shape, oct_shape, oct_shape, block, block, shape((64, 256))],
        (xy, features, voxel_mask, coarse_grad, conv_weight, down_weight), "shhhhh",
        scratch=[
            pltpu.VMEM((2, 2, 32, PLANE), BF16), pltpu.VMEM((2, 2, PLANE), I32),
            pltpu.VMEM((2, 2, 64, HALF * PLANE), BF16), pltpu.VMEM((32, 864), BF16), pltpu.VMEM((64, 256), BF16),
            pltpu.SemaphoreType.DMA((8,)),
        ],
        us=2, vmem_mib=58,
    )
    core_side = exchange(core_edge, 0)
    cross_side = exchange_cross(cross_edge)
    arrived = exchange(away, 0)
    acc_shape = shape((20 * 32, PLANE), F32)
    cols = pltpu.VMEM((16 * 288, PLANE), BF16)
    two_cols = pltpu.VMEM((2, 16 * 288, PLANE), BF16)
    mask = pltpu.VMEM((2, voxels), I32)
    windows = pltpu.VMEM((2, 9, 32, PLANE), BF16)
    all_cols, acc = call(
        inner_kernel, "forward_own_planes",
        [shape((2, 16 * 288, PLANE)), shape((2, 4096, PLANE), F32)],
        (xy, features, voxel_mask, stacked), "shhh", out_kinds="hh",
        scratch=[
            pltpu.VMEM((2, 32, voxels), BF16), mask, pltpu.VMEM((96, 288), BF16), pltpu.VMEM((2, 2, 9, 32, PLANE), BF16), pltpu.VMEM((512, 512), BF16),
            two_cols, pltpu.VMEM((2, 20 * 32, PLANE), F32), pltpu.SemaphoreType.DMA((7,)),
        ],
        us=5, vmem_mib=58,
    )
    octants, gplanes, gcore, gcross, sums = call(
        functools.partial(outer_kernel, layers, scale), "forward_rest",
        [oct_shape, shape((512, 512)), side_shape, side_shape, shape((32, 1408), F32)],
        (xy, all_cols, acc, voxel_mask, down_weight, core_side, cross_side, own, arrived, stacked, down_t), "shhhhvvvvvv",
        scratch=[
            two_cols, pltpu.VMEM((2, 512, PLANE), F32), mask, pltpu.VMEM((64, 256), BF16),
            pltpu.VMEM((512, 512), BF16), pltpu.VMEM((2, HALF, 256, PLANE), BF16), pltpu.VMEM((256, 1024), BF16),
            pltpu.VMEM((2, 20 * 32, PLANE), BF16), pltpu.VMEM((96, 288), F32), pltpu.SemaphoreType.DMA((4,)),
        ],
        us=6, vmem_mib=50,
    )
    odd = lax.axis_index("morton") % 2
    rows = sums.shape[0] // 2
    keep = lax.dynamic_slice_in_dim(sums, odd * rows, rows, 0)
    total = keep + exchange(lax.dynamic_slice_in_dim(sums, (1 - odd) * rows, rows, 0), 0)
    gcore_side = exchange(gcore, 0)
    octants_there = exchange(octants, 0)
    gcross_side = exchange_cross(gcross)
    back = []
    for bit in range(1, rounds):
        step = exchange(total, bit)
        if bit in (1, 2):
            back.append(
                call(
                    functools.partial(back_inner_kernel, bit - 1), "backward_own_planes", acc_shape,
                    (xy, total, gplanes, flipped), "shvv", scratch=[windows, cols], us=3,
                )
            )
        if bit == 3:
            input_grad = call(
                functools.partial(back_outer_kernel, layers), "backward_rest", shape((bricks, channels, voxels)),
                (xy, voxel_mask, total, *back, gcore_side, gcross_side, flipped), "shhvvvvv",
                scratch=[mask, pltpu.VMEM((2, 512, PLANE), F32), pltpu.SemaphoreType.DMA((1,))], us=2,
            )
        total = total + step
    other = exchange(total, 0)
    coarse_out = call(
        coarse_kernel, "place", shape((2, 64, voxels)), (xy, octants, octants_there, total), "svvh", us=2
    )
    conv_grad, down_grad = call(
        finish_kernel, "finish", [shape((32, 864), F32), shape((64, 256), F32)], (total, other), "vv"
    )
    return coarse_out, input_grad, conv_grad, down_grad


def solution(mesh):
    return jax.shard_map(
        per_device,
        mesh=mesh,
        in_specs=(
            P(("groups", "morton"), None, None),
            P(("groups", "morton"), None),
            P("groups", None),
            P(("groups", "morton"), None),
            P(),
            P(),
            P(("groups", "morton"), None, None),
        ),
        out_specs=(
            P(("groups", "morton"), None, None),
            P(("groups", "morton"), None, None),
            P("groups", None),
            P("groups", None),
        ),
        check_vma=False,
    )
```

time: 60.9 us -> 43.4 us (0.71)
  waiting for transfers between devices: 10.4 us -> 1.04 us
  local copies, waits for them, and re-layouts: 5.97 us -> 0.06 us
  starting transfers between devices: 20.7 us -> 17.7 us
  Pallas kernels: 21.9 us -> 23.2 us
  other arithmetic: 0.7 us -> 0.06 us
    ppermute x4 -> x2, starting transfers between devices: 13.9 us -> 7.63 us  [exchange_cross(): lax.ppermute(value, 'morton', pairs + [(target, source) for source, targe...]
    ppermute x7 -> x9, waiting for transfers between devices: 6.2 us -> 1.04 us  [exchange(): lax.ppermute(value, 'morton', [(i, i ^ 1 << bit) for i in range(lax.axis_...]
    ppermute x4 -> x2, waiting for transfers between devices: 4.18 us -> 0.01 us  [exchange_cross(): lax.ppermute(value, 'morton', pairs + [(target, source) for source, targe...]
    unnamed x16 -> x14, local copies, waits for them, and re-layouts: 3.92 us -> 0.04 us
    ppermute x7 -> x9, starting transfers between devices: 6.76 us -> 10.1 us  [exchange(): lax.ppermute(value, 'morton', [(i, i ^ 1 << bit) for i in range(lax.axis_...]
    pallas_call x4 -> x8, Pallas kernels: 21.9 us -> 23.2 us  [call(): pl.pallas_call(body, name=name, out_shape=out_shapes, in_specs=[specs[kin...]
    slice x2 -> x0, local copies, waits for them, and re-layouts: 0.66 us -> none  [the longest x1 0.65 us: per_device(): conv_grad = total[:, :864]]
    concatenate x1 -> x0, other arithmetic: 0.63 us -> none  [per_device(): down_grad = jnp.concatenate([total[:, 896:1152], total[:, 1152:]], axis=0)]
  transfers between devices with their start and end apart: 11 -> 11, of which waited for: 5 -> 2; matrix products, arithmetic and copies ran while one was open for 2% -> 0% of each run, Pallas kernels for 15% -> 31%
where the time goes in v1:
time: 43.4 us; the launch traced here: 42.9 us
  Pallas kernels  23.2 us (53%)
  starting transfers between devices  17.7 us (41%)
  waiting for transfers between devices  1.04 us (2%)
  between operations  0.9 us (2%)
    pallas_call x8, Pallas kernels, call(): pl.pallas_call(body, name=name, out_shape=out_shapes, in_specs=[specs[kin...  23.2 us
    ppermute x9, starting transfers between devices, exchange(): lax.ppermute(value, 'morton', [(i, i ^ 1 << bit) for i in range(lax.axis_...  10.1 us
    ppermute x2, starting transfers between devices, exchange_cross(): lax.ppermute(value, 'morton', pairs + [(target, source) for source, targe...  7.63 us
    ppermute x9, waiting for transfers between devices, exchange(): lax.ppermute(value, 'morton', [(i, i ^ 1 << bit) for i in range(lax.axis_...  1.04 us
  transfers between devices with their start and end apart: 11, of which 2 were waited for; matrix products, arithmetic and copies ran while one was open for 0% of the time, Pallas kernels for 31%

profile of v1, /device:TPU:1, one launch (start us, length us, event | category | flops | bytes accessed | tf_op | source)
XLA Modules:
  0.0 42.9 jit_solution(16469371967243528251)
XLA Ops:
  0.6 3.5 %prepare.1 = (bf16[32,512]{1,0:T(8,128)(2,1)}, bf16[32,512]{1,0:T(8,128)(2,1)}, bf16[64,1024]{1,0:T(8,128)(2,1)}, bf16[64,1024]{1,0:T(8,128)(2,1)}, bf16[96,288]...) custom-call(s32[2,32]{1,0:T(2,128)} %bitcast.1, bf16[2,32,4096]{2,1,0:T(8,128)(2,1)} %feat_hbm.3, ...), custom_call_target="tpu_custom_call" | custom-call | flops 2000000000 | bytes 7000000 | tf_op jit(solution)/shard_map/prepare/pallas_call | solution.py:349
  4.1 0.1 collective-permute-start.2
  4.2 0.5 %collective-permute-start = (bf16[32,512]{1,0:T(8,128)(2,1)}, bf16[32,512]{1,0:T(8,128)(2,1)S(1)}, u32[]{:S(2)}, u32[]{:S(2)}) collective-permute-start(bf16[32,512]{1,0:T(8,128)(2,1)} %get-tuple-element.23), channel_id=1, source_target_pairs={{0,1},{1,0},{2,3},{3,2},{4,5},{5,4},{6,7},{7,6},{8,9},{9,8},{10,11... | collective-permute-start | bytes 98312 | tf_op jit(solution)/shard_map/ppermute | solution.py:366
  4.7 4.5 %collective-permute-start.1 = (bf16[32,512]{1,0:T(8,128)(2,1)}, bf16[32,512]{1,0:T(8,128)(2,1)S(1)}, u32[]{:S(2)}, u32[]{:S(2)}) collective-permute-start(bf16[32,512]{1,0:T(8,128)(2,1)} %get-tuple-element.24), channel_id=1, source_target_pairs={{1,2},{3,4},{5,6},{7,8},{9,10},{11,12},{13,14},{2,1},{4,3},{6,5},{... | collective-permute-start | bytes 98312 | tf_op jit(solution)/shard_map/ppermute | solution.py:372
  9.2 0.0 copy-start
  9.2 0.0 copy-start.1
  9.2 0.0 copy-start.2
  9.2 0.0 copy-start.3
  9.2 0.0 copy-start.5
  9.3 0.0 copy-start.6
  9.3 5.8 %forward_own_planes.1 = (bf16[2,4608,256]{2,1,0:T(8,128)(2,1)}, f32[2,4096,256]{2,1,0:T(8,128)}) custom-call(s32[2,32]{1,0:T(2,128)} %bitcast.2, bf16[2,32,4096]{2,1,0:T(8,128)(2,1)} %feat_hbm.3, s32[2,4096]{1,0:T(2,128)} %mask_hbm.7, bf16[96,288]{1,0:T(8,128)(2,1)} %get-tuple-element.20.stacked_hbm.stacked_ref), custom_call_target="tpu_custom_call" | custom-call | flops 5000000000 | bytes 17500000 | tf_op jit(solution)/shard_map/forward_own_planes/pallas_call | solution.py:349
  15.1 0.0 collective-permute-done.core_ref
  15.1 0.0 collective-permute-done.1.cross_ref
  15.1 0.0 collective-permute-done.2.recv_ref
  15.1 0.0 copy-done
  15.1 0.0 copy-done.1
  15.1 0.0 copy-done.2
  15.1 0.0 copy-done.3
  15.1 0.0 copy-done.5
  15.2 0.0 copy-done.6
  15.2 0.0 copy-start.4
  15.2 5.9 %forward_rest.1 = (bf16[64,1024]{1,0:T(8,128)(2,1)S(1)}, bf16[512,512]{1,0:T(8,128)(2,1)S(1)}, bf16[32,512]{1,0:T(8,128)(2,1)S(1)}, bf16[32,512]{1,0:T(8,128)(2,1)S(1)}, f32[32,1408]{1,0:T(8,128)S(1)}) custom-call(s32[2,32]{1,0:T(2,128)S(1)} %bitcast.3, bf16[2,4608,256]{2,1,0:T(8,128)(2,1)} %get-tuple-element.21.cols_hbm, ...), custom_call_target="tpu_custom_call" | custom-call | flops 6000000000 | bytes 21000000 | tf_op jit(solution)/shard_map/forward_rest/pallas_call | solution.py:349
  21.1 0.1 collective-permute-start.4
  21.2 0.5 %collective-permute-start.8 = (bf16[32,512]{1,0:T(8,128)(2,1)S(1)}, bf16[32,512]{1,0:T(8,128)(2,1)S(1)}, u32[]{:S(2)}, u32[]{:S(2)}) collective-permute-start(bf16[32,512]{1,0:T(8,128)(2,1)S(1)} %get-tuple-element.32), channel_id=1, source_target_pairs={{0,1},{1,0},{2,3},{3,2},{4,5},{5,4},{6,7},{7,6},{8,9},{9,8},{10,11... | collective-permute-start | bytes 98312 | tf_op jit(solution)/shard_map/ppermute | solution.py:366
  21.7 3.1 %collective-permute-start.9 = (bf16[32,512]{1,0:T(8,128)(2,1)S(1)}, bf16[32,512]{1,0:T(8,128)(2,1)S(1)}, u32[]{:S(2)}, u32[]{:S(2)}) collective-permute-start(bf16[32,512]{1,0:T(8,128)(2,1)S(1)} %get-tuple-element.33), channel_id=1, source_target_pairs={{1,2},{3,4},{5,6},{7,8},{9,10},{11,12},{13,14},{2,1},{4,3},{6,5},{... | collective-permute-start | bytes 98312 | tf_op jit(solution)/shard_map/ppermute | solution.py:372
  24.8 0.1 collective-permute-start.3
  24.9 0.0 collective-permute-done.4
  24.9 1.3 %collective-permute-start.5 = (f32[16,1408]{1,0:T(8,128)S(1)}, f32[16,1408]{1,0:T(8,128)S(1)}, u32[]{:S(2)}, u32[]{:S(2)}) collective-permute-start(f32[16,1408]{1,0:T(8,128)S(1)} %dynamic-slice_add_fusion.after_ref), channel_id=1, source_target_pairs={{0,2},{1,3},{2,0},{3,1},{4,6},{5,7},{6,4},{7,5},{8,10},{9,11},{10,... | collective-permute-start | bytes 270344 | tf_op jit(solution)/shard_map/ppermute | solution.py:366
  26.2 0.0 copy-done.4
  26.3 1.7 %backward_own_planes.2.acc0_ref = f32[640,256]{1,0:T(8,128)S(1)} custom-call(s32[2,32]{1,0:T(2,128)S(1)} %bitcast.4, f32[16,1408]{1,0:T(8,128)S(1)} %dynamic-slice_add_fusion.after_ref, bf16[512,512]{1,0:T(8,128)(2,1)S(1)} %get-tuple-element.30.gplanes_ref, bf16[96,288]{1,0:T(8,128)(2,1)S(1)} %copy-done.4), custom_call_target="tpu_custom_call" | custom-call | flops 3000000000 | bytes 10500000 | tf_op jit(solution)/shard_map/backward_own_planes/pallas_call | solution.py:349
  27.9 0.8 %collective-permute-done.5 = f32[16,1408]{1,0:T(8,128)S(1)} collective-permute-done((f32[16,1408]{1,0:T(8,128)S(1)}, f32[16,1408]{1,0:T(8,128)S(1)}, u32[]{:S(2)}, u32[]{:S(2)}) %collective-permute-start.5) | collective-permute-done | bytes 90144 | tf_op jit(solution)/shard_map/ppermute | solution.py:366
  28.7 2.0 %collective-permute-start.6 = (f32[16,1408]{1,0:T(8,128)S(1)}, f32[16,1408]{1,0:T(8,128)S(1)}, u32[]{:S(2)}, u32[]{:S(2)}) collective-permute-start(f32[16,1408]{1,0:T(8,128)S(1)} %add.26.after_ref), channel_id=1, source_target_pairs={{0,4},{1,5},{2,6},{3,7},{4,0},{5,1},{6,2},{7,3},{8,12},{9,13},{10,... | collective-permute-start | bytes 270344 | tf_op jit(solution)/shard_map/ppermute | solution.py:366
  30.7 1.7 %backward_own_planes.3.acc1_ref = f32[640,256]{1,0:T(8,128)S(1)} custom-call(s32[2,32]{1,0:T(2,128)S(1)} %bitcast.5, f32[16,1408]{1,0:T(8,128)S(1)} %add.26.after_ref, bf16[512,512]{1,0:T(8,128)(2,1)S(1)} %get-tuple-element.30.gplanes_ref, bf16[96,288]{1,0:T(8,128)(2,1)S(1)} %copy-done.4), custom_call_target="tpu_custom_call" | custom-call | flops 3000000000 | bytes 10500000 | tf_op jit(solution)/shard_map/backward_own_planes/pallas_call | solution.py:349
  32.4 0.2 collective-permute-done.6
  32.6 2.6 %collective-permute-start.7 = (f32[16,1408]{1,0:T(8,128)S(1)}, f32[16,1408]{1,0:T(8,128)S(1)}, u32[]{:S(2)}, u32[]{:S(2)}) collective-permute-start(f32[16,1408]{1,0:T(8,128)S(1)} %add.27.after_ref), channel_id=1, source_target_pairs={{0,8},{1,9},{2,10},{3,11},{4,12},{5,13},{6,14},{7,15},{8,0},{9,1},... | collective-permute-start | bytes 270344 | tf_op jit(solution)/shard_map/ppermute | solution.py:366
  35.2 0.0 collective-permute-done.8.core_ref
  35.2 0.0 collective-permute-done.9.cross_ref
  35.2 2.0 %backward_rest.1 = bf16[2,32,4096]{2,1,0:T(8,128)(2,1)} custom-call(s32[2,32]{1,0:T(2,128)S(1)} %bitcast.6, s32[2,4096]{1,0:T(2,128)S(1)} %copy-done.1, f32[16,1408]{1,0:T(8,128)S(1)} %add.27.after_ref, f32[640,256]{1,0:T(8,128)S(1)} %backward_own_planes.2.acc0_ref, f32[640,256]{1,0:T(8,128)S(1)} %backward_own_planes.3.acc1_ref, ...), custom_call_target="tpu_custom_call" | custom-call | flops 2000000000 | bytes 7000000 | tf_op jit(solution)/shard_map/backward_rest/pallas_call | solution.py:349
  37.2 0.0 collective-permute-done.7
  37.2 3.0 %collective-permute-start.10 = (f32[16,1408]{1,0:T(8,128)S(1)}, f32[16,1408]{1,0:T(8,128)S(1)}, u32[]{:S(2)}, u32[]{:S(2)}) collective-permute-start(f32[16,1408]{1,0:T(8,128)S(1)} %add.28.after_ref.total_ref), channel_id=1, source_target_pairs={{0,1},{1,0},{2,3},{3,2},{4,5},{5,4},{6,7},{7,6},{8,9},{9,8},{10,11... | collective-permute-start | bytes 270344 | tf_op jit(solution)/shard_map/ppermute | solution.py:366
  40.2 0.0 collective-permute-done.3.recv_ref
  40.2 2.0 %place.1 = bf16[2,64,4096]{2,1,0:T(8,128)(2,1)} custom-call(s32[2,32]{1,0:T(2,128)S(1)} %bitcast.7, bf16[64,1024]{1,0:T(8,128)(2,1)S(1)} %get-tuple-element.28.own_ref, bf16[64,1024]{1,0:T(8,128)(2,1)S(1)} %collective-permute-done.3.recv_ref, f32[16,1408]{1,0:T(8,128)S(1)} %add.28.after_ref.total_ref), custom_call_target="tpu_custom_call" | custom-call | flops 2000000000 | bytes 7000000 | tf_op jit(solution)/shard_map/place/pallas_call | solution.py:349
  42.2 0.0 collective-permute-done.10.other_ref
  42.2 0.7 %finish.1 = (f32[32,864]{1,0:T(8,128)}, f32[64,256]{1,0:T(8,128)}) custom-call(f32[16,1408]{1,0:T(8,128)S(1)} %add.28.after_ref.total_ref, f32[16,1408]{1,0:T(8,128)S(1)} %collective-permute-done.10.other_ref), custom_call_target="tpu_custom_call" | custom-call | flops 1000000000 | bytes 3500000 | tf_op jit(solution)/shard_map/finish/pallas_call | solution.py:349
  (5 shorter events, 0.1 us)
Async XLA Ops:
  4.1 11.0 %collective-permute-start.2 = (bf16[64,1024]{1,0:T(8,128)(2,1)}, bf16[64,1024]{1,0:T(8,128)(2,1)S(1)}, u32[]{:S(2)}, u32[]{:S(2)}) collective-permute-start(bf16[64,1024]{1,0:T(8,128)(2,1)} %get-tuple-element.26), channel_id=1, source_target_pairs={{0,1},{1,0},{2,3},{3,2},{4,5},{5,4},{6,7},{7,6},{8,9},{9,8},{10,11... | collective-permute-start | bytes 393224 | tf_op jit(solution)/shard_map/ppermute | solution.py:366
  4.2 10.9 %collective-permute-start = (bf16[32,512]{1,0:T(8,128)(2,1)}, bf16[32,512]{1,0:T(8,128)(2,1)S(1)}, u32[]{:S(2)}, u32[]{:S(2)}) collective-permute-start(bf16[32,512]{1,0:T(8,128)(2,1)} %get-tuple-element.23), channel_id=1, source_target_pairs={{0,1},{1,0},{2,3},{3,2},{4,5},{5,4},{6,7},{7,6},{8,9},{9,8},{10,11... | collective-permute-start | bytes 98312 | tf_op jit(solution)/shard_map/ppermute | solution.py:366
  4.7 10.4 %collective-permute-start.1 = (bf16[32,512]{1,0:T(8,128)(2,1)}, bf16[32,512]{1,0:T(8,128)(2,1)S(1)}, u32[]{:S(2)}, u32[]{:S(2)}) collective-permute-start(bf16[32,512]{1,0:T(8,128)(2,1)} %get-tuple-element.24), channel_id=1, source_target_pairs={{1,2},{3,4},{5,6},{7,8},{9,10},{11,12},{13,14},{2,1},{4,3},{6,5},{... | collective-permute-start | bytes 98312 | tf_op jit(solution)/shard_map/ppermute | solution.py:372
  9.2 5.9 %copy-start = (bf16[64,256]{1,0:T(8,128)(2,1)S(1)}, bf16[64,256]{1,0:T(8,128)(2,1)}, u32[]{:S(2)}) copy-start(bf16[64,256]{1,0:T(8,128)(2,1)} %down_hbm.3) | copy-start | bytes 98308
  9.2 5.9 %copy-start.1 = (s32[2,4096]{1,0:T(2,128)S(1)}, s32[2,4096]{1,0:T(2,128)}, u32[]{:S(2)}) copy-start(s32[2,4096]{1,0:T(2,128)} %mask_hbm.7) | copy-start | bytes 98308
  9.2 5.9 %copy-start.2 = (s32[32,2]{0,1:T(2,128)S(1)}, s32[32,2]{0,1:T(2,128)}, u32[]{:S(2)}) copy-start(s32[32,2]{0,1:T(2,128)} %param.9) | copy-start | bytes 772
  9.2 5.9 %copy-start.3 = (bf16[64,1024]{1,0:T(8,128)(2,1)S(1)}, bf16[64,1024]{1,0:T(8,128)(2,1)}, u32[]{:S(2)}) copy-start(bf16[64,1024]{1,0:T(8,128)(2,1)} %get-tuple-element.25.own_ref) | copy-start | bytes 393220
  9.2 5.9 %copy-start.5 = (bf16[96,288]{1,0:T(8,128)(2,1)S(1)}, bf16[96,288]{1,0:T(8,128)(2,1)}, u32[]{:S(2)}) copy-start(bf16[96,288]{1,0:T(8,128)(2,1)} %get-tuple-element.20.stacked_hbm.stacked_ref) | copy-start | bytes 165892
  9.3 5.9 %copy-start.6 = (bf16[64,256]{1,0:T(8,128)(2,1)S(1)}, bf16[64,256]{1,0:T(8,128)(2,1)}, u32[]{:S(2)}) copy-start(bf16[64,256]{1,0:T(8,128)(2,1)} %get-tuple-element.27.down_t_ref) | copy-start | bytes 98308
  15.2 11.1 %copy-start.4 = (bf16[96,288]{1,0:T(8,128)(2,1)S(1)}, bf16[96,288]{1,0:T(8,128)(2,1)}, u32[]{:S(2)}) copy-start(bf16[96,288]{1,0:T(8,128)(2,1)} %get-tuple-element.31.flipped_ref) | copy-start | bytes 165892
  21.1 3.8 %collective-permute-start.4 = (f32[16,1408]{1,0:T(8,128)S(1)}, f32[16,1408]{1,0:T(8,128)S(1)}, u32[]{:S(2)}, u32[]{:S(2)}) collective-permute-start(f32[16,1408]{1,0:T(8,128)S(1)} %constant_dynamic-slice_fusion), channel_id=1, source_target_pairs={{0,1},{1,0},{2,3},{3,2},{4,5},{5,4},{6,7},{7,6},{8,9},{9,8},{10,11... | collective-permute-start | bytes 270344 | tf_op jit(solution)/shard_map/ppermute | solution.py:366
  21.2 14.0 %collective-permute-start.8 = (bf16[32,512]{1,0:T(8,128)(2,1)S(1)}, bf16[32,512]{1,0:T(8,128)(2,1)S(1)}, u32[]{:S(2)}, u32[]{:S(2)}) collective-permute-start(bf16[32,512]{1,0:T(8,128)(2,1)S(1)} %get-tuple-element.32), channel_id=1, source_target_pairs={{0,1},{1,0},{2,3},{3,2},{4,5},{5,4},{6,7},{7,6},{8,9},{9,8},{10,11... | collective-permute-start | bytes 98312 | tf_op jit(solution)/shard_map/ppermute | solution.py:366
  21.7 13.5 %collective-permute-start.9 = (bf16[32,512]{1,0:T(8,128)(2,1)S(1)}, bf16[32,512]{1,0:T(8,128)(2,1)S(1)}, u32[]{:S(2)}, u32[]{:S(2)}) collective-permute-start(bf16[32,512]{1,0:T(8,128)(2,1)S(1)} %get-tuple-element.33), channel_id=1, source_target_pairs={{1,2},{3,4},{5,6},{7,8},{9,10},{11,12},{13,14},{2,1},{4,3},{6,5},{... | collective-permute-start | bytes 98312 | tf_op jit(solution)/shard_map/ppermute | solution.py:372
  24.8 15.4 %collective-permute-start.3 = (bf16[64,1024]{1,0:T(8,128)(2,1)S(1)}, bf16[64,1024]{1,0:T(8,128)(2,1)S(1)}, u32[]{:S(2)}, u32[]{:S(2)}) collective-permute-start(bf16[64,1024]{1,0:T(8,128)(2,1)S(1)} %get-tuple-element.28.own_ref), channel_id=1, source_target_pairs={{0,1},{1,0},{2,3},{3,2},{4,5},{5,4},{6,7},{7,6},{8,9},{9,8},{10,11... | collective-permute-start | bytes 393224 | tf_op jit(solution)/shard_map/ppermute | solution.py:366
  24.9 3.8 %collective-permute-start.5 = (f32[16,1408]{1,0:T(8,128)S(1)}, f32[16,1408]{1,0:T(8,128)S(1)}, u32[]{:S(2)}, u32[]{:S(2)}) collective-permute-start(f32[16,1408]{1,0:T(8,128)S(1)} %dynamic-slice_add_fusion.after_ref), channel_id=1, source_target_pairs={{0,2},{1,3},{2,0},{3,1},{4,6},{5,7},{6,4},{7,5},{8,10},{9,11},{10,... | collective-permute-start | bytes 270344 | tf_op jit(solution)/shard_map/ppermute | solution.py:366
  28.7 3.9 %collective-permute-start.6 = (f32[16,1408]{1,0:T(8,128)S(1)}, f32[16,1408]{1,0:T(8,128)S(1)}, u32[]{:S(2)}, u32[]{:S(2)}) collective-permute-start(f32[16,1408]{1,0:T(8,128)S(1)} %add.26.after_ref), channel_id=1, source_target_pairs={{0,4},{1,5},{2,6},{3,7},{4,0},{5,1},{6,2},{7,3},{8,12},{9,13},{10,... | collective-permute-start | bytes 270344 | tf_op jit(solution)/shard_map/ppermute | solution.py:366
  32.6 4.6 %collective-permute-start.7 = (f32[16,1408]{1,0:T(8,128)S(1)}, f32[16,1408]{1,0:T(8,128)S(1)}, u32[]{:S(2)}, u32[]{:S(2)}) collective-permute-start(f32[16,1408]{1,0:T(8,128)S(1)} %add.27.after_ref), channel_id=1, source_target_pairs={{0,8},{1,9},{2,10},{3,11},{4,12},{5,13},{6,14},{7,15},{8,0},{9,1},... | collective-permute-start | bytes 270344 | tf_op jit(solution)/shard_map/ppermute | solution.py:366
  37.2 5.0 %collective-permute-start.10 = (f32[16,1408]{1,0:T(8,128)S(1)}, f32[16,1408]{1,0:T(8,128)S(1)}, u32[]{:S(2)}, u32[]{:S(2)}) collective-permute-start(f32[16,1408]{1,0:T(8,128)S(1)} %add.28.after_ref.total_ref), channel_id=1, source_target_pairs={{0,1},{1,0},{2,3},{3,2},{4,5},{5,4},{6,7},{7,6},{8,9},{9,8},{10,11... | collective-permute-start | bytes 270344 | tf_op jit(solution)/shard_map/ppermute | solution.py:366

commit v2 on v1

--- a/solution.py
+++ b/solution.py
@@ -57,7 +57,7 @@
 
 def prepare_kernel(
     xy_ref, feat_hbm, mask_hbm, grad_hbm, weight_hbm, down_hbm,
-    core_ref, cross_ref, own_ref, send_ref, flipped_ref, stacked_ref, down_t_ref,
+    send_ref, cross_ref, own_ref, flipped_ref, stacked_ref, down_t_ref,
     feat_ref, mask_ref, grad_ref, weight_ref, down_ref, sems,
 ):
     layer = lax.axis_index("morton")
@@ -67,44 +67,42 @@
         grad_hbm.at[:, :, pl.ds(pl.multiple_of(half * HALF * PLANE, HALF * PLANE), HALF * PLANE)]
         for half in (1 - parity, parity)
     ]
-    copies = start_all(
-        ((halves[0], grad_ref.at[0]), (halves[1], grad_ref.at[1]), (weight_hbm, weight_ref), (down_hbm, down_ref)), sems
-    )
-    edges = []
+    pairs = [(weight_hbm, weight_ref), (down_hbm, down_ref)]
     for side in range(2):
         z = jnp.where(parity == side, EDGE - 1, 0)
         lanes = pl.ds(pl.multiple_of(z * PLANE, PLANE), PLANE)
-        edges += start_all(
-            ((feat_hbm.at[:, :, lanes], feat_ref.at[side]), (mask_hbm.at[:, lanes], mask_ref.at[side])),
-            sems.at[pl.ds(4 + 2 * side, 2)],
-        )
+        pairs += [(feat_hbm.at[:, :, lanes], feat_ref.at[side]), (mask_hbm.at[:, lanes], mask_ref.at[side])]
+    pairs += [(halves[0], grad_ref.at[0]), (halves[1], grad_ref.at[1])]
+    copies = start_all(pairs, sems)
     row = iota((2 * PLANE, 2 * QUARTER), 0)
     lane = iota((2 * PLANE, 2 * QUARTER), 1)
     picks = [one_hot(row, octant_key(xy_ref, target, parity, lane)) for target in (partner, layer)]
-    for copy in edges:
-        copy.wait()
-    for side, ref in enumerate((core_ref, cross_ref)):
+    for copy in copies[:2]:
+        copy.wait()
+    flipped = weight_ref[...].astype(F32).T.astype(BF16)
+    for dz in range(3):
+        rows = pl.ds(dz * 32, 32)
+        blocks = [flipped[j * 32 : (j + 1) * 32] for j in (26 - dz * 9 - s for s in range(9))]
+        flipped_ref[rows, :] = jnp.concatenate(blocks, axis=1)
+        stacked_ref[rows, :] = weight_ref[:, pl.ds(dz * 288, 288)]
+    down_t = down_ref[...].astype(F32).T.astype(BF16)
+    for kz in range(2):
+        blocks = [down_t[(kz * 4 + k) * 32 : (kz * 4 + k + 1) * 32] for k in range(4)]
+        down_t_ref[pl.ds(kz * 32, 32), :] = jnp.concatenate(blocks, axis=1)
+    for copy in copies[2:6]:
+        copy.wait()
+    for side, ref in enumerate((send_ref.at[pl.ds(64, 32)], cross_ref)):
         for r in range(2):
             mask = mask_ref[side, pl.ds(r, 1), :].astype(F32).astype(BF16)
             ref[:, pl.ds(r * PLANE, PLANE)] = feat_ref[side, r] * mask
-    for i, ref in enumerate((send_ref, own_ref)):
-        copies[i].wait()
+    for i, ref in enumerate((send_ref.at[pl.ds(0, 64)], own_ref)):
+        copies[6 + i].wait()
+        planes = [
+            jnp.concatenate([grad_ref[i, q, :, pl.ds(wz * PLANE, PLANE)] for q in range(2)], axis=1) for wz in range(HALF)
+        ]
+        found = mm(jnp.concatenate(planes, axis=0), picks[i]).astype(BF16)
         for wz in range(HALF):
-            lanes = pl.ds(wz * PLANE, PLANE)
-            planes = jnp.concatenate([grad_ref[i, 0, :, lanes], grad_ref[i, 1, :, lanes]], axis=1)
-            ref[:, pl.ds(wz * 2 * QUARTER, 2 * QUARTER)] = mm(planes, picks[i]).astype(BF16)
-    copies[2].wait()
-    copies[3].wait()
-    turned = weight_ref[...].astype(F32).T.astype(BF16)
-    for dz in range(3):
-        rows = pl.ds(dz * 32, 32)
-        blocks = [turned[j * 32 : (j + 1) * 32] for j in (26 - dz * 9 - s for s in range(9))]
-        flipped_ref[rows, :] = jnp.concatenate(blocks, axis=1)
-        stacked_ref[rows, :] = weight_ref[:, pl.ds(dz * 288, 288)]
-    turned = down_ref[...].astype(F32).T.astype(BF16)
-    for kz in range(2):
-        blocks = [turned[(kz * 4 + k) * 32 : (kz * 4 + k + 1) * 32] for k in range(4)]
-        down_t_ref[pl.ds(kz * 32, 32), :] = jnp.concatenate(blocks, axis=1)
+            ref[:, pl.ds(wz * 2 * QUARTER, 2 * QUARTER)] = found[wz * 64 : (wz + 1) * 64]
 
 
 def window_mask(shift, ox, oy):
@@ -134,21 +132,25 @@
     return pltpu.roll(both, back, 1) if back else both
 
 
-def build_masks(xy_ref, layer, r, mask_ref):
-    ox, oy = offset_of(xy_ref, layer, r, layer, 1 - r)
-    for shift in range(9):
-        mask_ref[0, shift] = window_mask(shift, 0, 0)
-        mask_ref[1, shift] = window_mask(shift, ox, oy)
-    return ox
-
-
-def unfold_planes(planes_ref, r, ox, mask_ref, cols_ref):
-    for p in range(0, EDGE, STEP):
+def build_masks(ox, oy, rows_ref, mask_ref):
+    shift = iota((16, PLANE), 0)
+    dy = (shift >= 3).astype(I32) + (shift >= 6).astype(I32) - 1
+    dx = shift - 3 * dy - 4
+    voxel = (iota((16, PLANE), 1) - (EDGE * dy + dx)) & (PLANE - 1)
+    x = (voxel & (EDGE - 1)) + dx - EDGE * ox
+    y = (voxel >> 4) + dy - EDGE * oy
+    rows_ref[...] = jnp.where(((x | y) & -EDGE) == 0, 1.0, 0.0)
+    for s in range(9):
+        mask_ref[s] = jnp.broadcast_to(rows_ref[pl.ds(s, 1), :], (32, PLANE)).astype(BF16)
+
+
+def unfold_planes(planes_ref, r, first, ox, own_ref, other_ref, cols_ref):
+    for p in range(first, first + STEP, STEP):
         rows = pl.ds(p * 32, STEP * 32)
         own = planes_ref[rows, pl.ds(r * PLANE, PLANE)]
         other = turned(planes_ref[rows, pl.ds((1 - r) * PLANE, PLANE)], ox)
         for shift in range(9):
-            piece = own if shift == 4 else shifted(own, other, (mask_ref[0, shift], mask_ref[1, shift]), shift)
+            piece = own if shift == 4 else shifted(own, other, (own_ref[shift], other_ref[shift]), shift)
             for q in range(STEP):
                 cols_ref[pl.ds((p + q) * 288 + shift * 32, 32), :] = piece[q * 32 : (q + 1) * 32]
 
@@ -172,11 +174,16 @@
 
 def inner_kernel(
     xy_ref, feat_hbm, mask_hbm, stacked_hbm, cols_hbm, acc_hbm,
-    feat_ref, mask_ref, stacked_ref, window_ref, in_ref, cols_ref, acc_ref, sems,
+    feat_ref, mask_ref, stacked_ref, rows_ref, window_ref, in_ref, cols_ref, acc_ref, sems,
 ):
     layer = lax.axis_index("morton")
     copies = start_all(((feat_hbm, feat_ref), (mask_hbm, mask_ref), (stacked_hbm, stacked_ref)), sems)
-    ox = [build_masks(xy_ref, layer, r, window_ref.at[r]) for r in range(2)]
+    build_masks(0, 0, rows_ref, window_ref.at[2])
+    ox = []
+    for r in range(2):
+        x, y = offset_of(xy_ref, layer, r, layer, 1 - r)
+        build_masks(x, y, rows_ref, window_ref.at[r])
+        ox.append(x)
     for copy in copies:
         copy.wait()
     for r in range(2):
@@ -186,11 +193,13 @@
             in_ref[pl.ds(z * 32, 32), pl.ds(r * PLANE, PLANE)] = feat_ref[r, :, lanes] * mask
     out = []
     for r in range(2):
-        unfold_planes(in_ref, r, ox[r], window_ref.at[r], cols_ref.at[r])
+        for i in range(2):
+            unfold_planes(in_ref, r, i * STEP, ox[r], window_ref.at[2], window_ref.at[r], cols_ref.at[r])
+            rows = pl.ds(i * STEP * 288, STEP * 288)
+            out += start_all(((cols_ref.at[r, rows], cols_hbm.at[r, rows]),), sems.at[pl.ds(5 + 2 * r + i, 1)])
+    for r in range(2):
         convolve(stacked_ref[...], cols_ref.at[r], acc_ref.at[r])
-        out += start_all(
-            ((cols_ref.at[r], cols_hbm.at[r]), (acc_ref.at[r, pl.ds(64, 512)], acc_hbm.at[r, pl.ds(0, 512)])), sems.at[pl.ds(3 + 2 * r, 2)]
-        )
+        out += start_all(((acc_ref.at[r, pl.ds(64, 512)], acc_hbm.at[r, pl.ds(0, 512)]),), sems.at[pl.ds(3 + r, 1)])
     for copy in out:
         copy.wait()
 
@@ -208,9 +217,9 @@
 
 
 def outer_kernel(
-    layers, scale, xy_ref, cols_hbm, acc_hbm, mask_hbm, down_hbm, core_ref, cross_ref, own_ref, recv_ref, stacked_ref, down_t_ref,
-    oct_ref, gplanes_ref, gcore_ref, gcross_ref, sums_ref,
-    cols_ref, acc_ref, mask_ref, down_ref, act_ref, up_ref, stride_ref, grad_ref, total_ref, sems,
+    layers, scale, xy_ref, cols_hbm, acc_hbm, mask_hbm, down_hbm, recv_ref, cross_ref, own_ref, stacked_ref, down_t_ref,
+    message_ref, gplanes_ref, gcross_ref, small_ref, sums_ref,
+    cols_ref, acc_ref, mask_ref, down_ref, gather_ref, act_ref, up_ref, stride_ref, grad_ref, total_ref, sems,
 ):
     copies = start_all(
         ((acc_hbm.at[:, pl.ds(0, 512)], acc_ref), (mask_hbm, mask_ref), (down_hbm, down_ref), (cols_hbm, cols_ref)), sems
@@ -218,7 +227,17 @@
     layer = lax.axis_index("morton")
     sides = sides_of(layer, layers)
 
-    grad_oct = own_ref[...] + recv_ref[...]
+    row = iota((2 * PLANE, PLANE), 0)
+    lane = iota((2 * PLANE, PLANE), 1)
+    row_key = (row >> 8) * 4096 + ((row >> 4) & 15) * 64 + (row & 15)
+    lane_key = ((lane >> 6) & 1) * 4096 + ((lane >> 3) & 7) * 128 + (lane & 7) * 2 + (lane >> 7)
+    for ky in range(2):
+        gather_ref[ky] = one_hot(row_key, lane_key + ky * 64)
+
+    core_ref = recv_ref.at[pl.ds(64, 32), pl.ds(0, 2 * PLANE)]
+    oct_ref = message_ref.at[pl.ds(0, 64)]
+    gcore_ref = message_ref.at[pl.ds(64, 32), pl.ds(0, 2 * PLANE)]
+    grad_oct = own_ref[...] + recv_ref[pl.ds(0, 64), :]
     pieces = jnp.concatenate([grad_oct[:, wz * 128 : (wz + 1) * 128] for wz in range(HALF)], axis=0)
     row = iota((128, PLANE), 0)
     lane = iota((128, PLANE), 1)
@@ -239,6 +258,7 @@
             side_cols.append(unfold_side(xy_ref, layer, r, other, ref[...]))
     for copy in copies[:3]:
         copy.wait()
+    small_ref[...] = mask_ref[...].astype(F32).astype(BF16)
     for side, (other, dz, z) in enumerate(sides):
         for r in range(2):
             acc_ref[r, rows_at(15 - z), :] += mm(stacked_ref[rows_at(dz), :], side_cols[side * 2 + r])
@@ -262,12 +282,8 @@
         for (other, dz, z), ref in zip(sides, (gcore_ref, gcross_ref)):
             ref[:, pl.ds(r * PLANE, PLANE)] = grad_ref[r, rows_at(17 - z), :]
 
-    row = iota((2 * PLANE, PLANE), 0)
-    lane = iota((2 * PLANE, PLANE), 1)
-    row_key = (row >> 8) * 4096 + ((row >> 4) & 15) * 64 + (row & 15)
-    lane_key = ((lane >> 6) & 1) * 4096 + ((lane >> 3) & 7) * 128 + (lane & 7) * 2 + (lane >> 7)
     for ky in range(2):
-        found = mm(act_ref[...], one_hot(row_key, lane_key + ky * 64)).astype(BF16)
+        found = mm(act_ref[...], gather_ref[ky]).astype(BF16)
         for z in range(EDGE):
             for kx in range(2):
                 rows = pl.ds((z % 2) * 128 + (ky * 2 + kx) * 32, 32)
@@ -290,31 +306,40 @@
     sums_ref[:, pl.ds(0, 896)] = jnp.concatenate([*total, jnp.zeros((32, 32), F32)], axis=1) * scale
 
 
-def back_inner_kernel(r, xy_ref, after_ref, gplanes_ref, flipped_ref, acc_ref, window_ref, cols_ref):
+def back_inner_kernel(xy_ref, after_ref, gplanes_ref, flipped_ref, acc_ref, rows_ref, window_ref, cols_ref):
     layer = lax.axis_index("morton")
-    ox = build_masks(xy_ref, layer, r, window_ref)
-    unfold_planes(gplanes_ref, r, ox, window_ref, cols_ref)
-    convolve(flipped_ref[...], cols_ref, acc_ref)
-
-
-def back_outer_kernel(
-    layers, xy_ref, mask_hbm, after_ref, acc0_ref, acc1_ref, core_ref, cross_ref, flipped_ref, out_ref,
-    mask_ref, sums_ref, sems,
-):
-    copies = start_all(((mask_hbm, mask_ref),), sems)
+    build_masks(0, 0, rows_ref, window_ref.at[0])
+    for r in range(2):
+        ox, oy = offset_of(xy_ref, layer, r, layer, 1 - r)
+        build_masks(ox, oy, rows_ref, window_ref.at[1 + r])
+        for i in range(2):
+            unfold_planes(gplanes_ref, r, i * STEP, ox, window_ref.at[0], window_ref.at[1 + r], cols_ref.at[r])
+        convolve(flipped_ref[...], cols_ref.at[r], acc_ref.at[r])
+
+
+def back_outer_kernel(layers, xy_ref, mask_ref, after_ref, acc_ref, recv_ref, cross_ref, flipped_ref, out_hbm, out_ref, sems):
+    core_ref = recv_ref.at[pl.ds(64, 32), pl.ds(0, 2 * PLANE)]
     layer = lax.axis_index("morton")
-    sides = sides_of(layer, layers)
-    for r, acc_ref in enumerate((acc0_ref, acc1_ref)):
-        sums_ref[r] = acc_ref[pl.ds(64, 512), :]
-        for (other, dz, z), ref in zip(sides, (core_ref, cross_ref)):
-            cols = unfold_side(xy_ref, layer, r, other, ref[...])
-            sums_ref[r, rows_at(15 - z), :] += mm(flipped_ref[rows_at(dz), :], cols)
-    copies[0].wait()
-    for r in range(2):
+    odd = layer % 2
+    out = []
+    for r in range(2):
+        terms = []
+        for (other, dz, z), ref in zip(sides_of(layer, layers), (core_ref, cross_ref)):
+            terms.append(mm(flipped_ref[rows_at(dz), :], unfold_side(xy_ref, layer, r, other, ref[...])))
+        below = jnp.where(odd == 1, terms[0], terms[1])
+        above = jnp.where(odd == 1, terms[1], terms[0])
         for z in range(EDGE):
             lanes = pl.ds(z * PLANE, PLANE)
             mask = mask_ref[pl.ds(r, 1), lanes].astype(F32)
-            out_ref[r, :, lanes] = (sums_ref[r, pl.ds((15 - z) * 32, 32), :] * mask).astype(BF16)
+            grad = acc_ref[r, pl.ds((17 - z) * 32, 32), :]
+            if z == 0:
+                grad = grad + below
+            if z == EDGE - 1:
+                grad = grad + above
+            out_ref[r, :, lanes] = (grad * mask).astype(BF16)
+        out += start_all(((out_ref.at[r], out_hbm.at[r]),), sems.at[pl.ds(r, 1)])
+    for copy in out:
+        copy.wait()
 
 
 def finish_kernel(total_ref, other_ref, conv_ref, down_ref):
@@ -326,19 +351,22 @@
         down_ref[pl.ds(pl.multiple_of(place * 16 + 32, 16), 16), :] = ref[:, pl.ds(1152, 256)]
 
 
-def coarse_kernel(xy_ref, own_ref, recv_ref, after_ref, out_ref):
+def coarse_kernel(xy_ref, own_ref, recv_ref, after_ref, out_hbm, out_ref, sems):
     layer = lax.axis_index("morton")
     parity = layer % 2
     partner = layer + 1 - 2 * parity
-    for target, half, ref in ((layer, parity, own_ref), (partner, 1 - parity, recv_ref)):
-        pieces = jnp.concatenate([ref[:, wz * 128 : (wz + 1) * 128] for wz in range(HALF)], axis=0)
-        key = octant_key(xy_ref, target, parity, iota((128, PLANE), 0))
+    out = []
+    for i, (target, half, ref) in enumerate(((layer, parity, own_ref), (partner, 1 - parity, recv_ref))):
+        pieces = jnp.concatenate([ref[:64, wz * 128 : (wz + 1) * 128] for wz in range(HALF)], axis=0)
+        key = octant_key(xy_ref, target, parity, iota((128, 2 * PLANE), 0))
+        placed = mm(pieces, one_hot(key, iota((128, 2 * PLANE), 1))).astype(BF16)
         for q in range(2):
-            lane = iota((128, PLANE), 1) + q * PLANE
-            placed = mm(pieces, one_hot(key, lane)).astype(BF16)
             for wz in range(HALF):
-                lanes = pl.ds(pl.multiple_of((half * HALF + wz) * PLANE, PLANE), PLANE)
-                out_ref[q, :, lanes] = placed[wz * 64 : (wz + 1) * 64]
+                out_ref[i, q, :, pl.ds(wz * PLANE, PLANE)] = placed[wz * 64 : (wz + 1) * 64, q * PLANE : (q + 1) * PLANE]
+        lanes = pl.ds(pl.multiple_of(half * HALF * PLANE, HALF * PLANE), HALF * PLANE)
+        out += start_all(((out_ref.at[i], out_hbm.at[:, :, lanes]),), sems.at[pl.ds(i, 1)])
+    for copy in out:
+        copy.wait()
 
 
 def call(body, name, out_shapes, operands, kinds, scratch=(), us=1, out_kinds=None, vmem_mib=24):
@@ -379,10 +407,11 @@
     scale = 1.0 / math.sqrt(bricks * layers * voxels)
     side_shape = shape((32, 2 * PLANE))
     oct_shape = shape((64, 1024))
+    message_shape = shape((96, 1024))
     xy = brick_xy.T
     block = shape((96, 288))
-    core_edge, cross_edge, own, away, flipped, stacked, down_t = call(
-        prepare_kernel, "prepare", [side_shape, side_shape, oct_shape, oct_shape, block, block, shape((64, 256))],
+    message, cross_edge, own, flipped, stacked, down_t = call(
+        prepare_kernel, "prepare", [message_shape, side_shape, oct_shape, block, block, shape((64, 256))],
         (xy, features, voxel_mask, coarse_grad, conv_weight, down_weight), "shhhhh",
         scratch=[
             pltpu.VMEM((2, 2, 32, PLANE), BF16), pltpu.VMEM((2, 2, PLANE), I32),
@@ -391,31 +420,30 @@
         ],
         us=2, vmem_mib=58,
     )
-    core_side = exchange(core_edge, 0)
+    arrived = exchange(message, 0)
     cross_side = exchange_cross(cross_edge)
-    arrived = exchange(away, 0)
-    acc_shape = shape((20 * 32, PLANE), F32)
-    cols = pltpu.VMEM((16 * 288, PLANE), BF16)
     two_cols = pltpu.VMEM((2, 16 * 288, PLANE), BF16)
     mask = pltpu.VMEM((2, voxels), I32)
-    windows = pltpu.VMEM((2, 9, 32, PLANE), BF16)
+    windows = pltpu.VMEM((3, 9, 32, PLANE), BF16)
+    mask_rows = pltpu.VMEM((16, PLANE), F32)
     all_cols, acc = call(
         inner_kernel, "forward_own_planes",
         [shape((2, 16 * 288, PLANE)), shape((2, 4096, PLANE), F32)],
         (xy, features, voxel_mask, stacked), "shhh", out_kinds="hh",
         scratch=[
-            pltpu.VMEM((2, 32, voxels), BF16), mask, pltpu.VMEM((96, 288), BF16), pltpu.VMEM((2, 2, 9, 32, PLANE), BF16), pltpu.VMEM((512, 512), BF16),
-            two_cols, pltpu.VMEM((2, 20 * 32, PLANE), F32), pltpu.SemaphoreType.DMA((7,)),
+            pltpu.VMEM((2, 32, voxels), BF16), mask, pltpu.VMEM((96, 288), BF16), mask_rows, windows,
+            pltpu.VMEM((512, 512), BF16),
+            two_cols, pltpu.VMEM((2, 20 * 32, PLANE), F32), pltpu.SemaphoreType.DMA((9,)),
         ],
         us=5, vmem_mib=58,
     )
-    octants, gplanes, gcore, gcross, sums = call(
+    message, gplanes, gcross, small_mask, sums = call(
         functools.partial(outer_kernel, layers, scale), "forward_rest",
-        [oct_shape, shape((512, 512)), side_shape, side_shape, shape((32, 1408), F32)],
-        (xy, all_cols, acc, voxel_mask, down_weight, core_side, cross_side, own, arrived, stacked, down_t), "shhhhvvvvvv",
+        [message_shape, shape((512, 512)), side_shape, shape((2, voxels)), shape((32, 1408), F32)],
+        (xy, all_cols, acc, voxel_mask, down_weight, arrived, cross_side, own, stacked, down_t), "shhhhvvvvv",
         scratch=[
             two_cols, pltpu.VMEM((2, 512, PLANE), F32), mask, pltpu.VMEM((64, 256), BF16),
-            pltpu.VMEM((512, 512), BF16), pltpu.VMEM((2, HALF, 256, PLANE), BF16), pltpu.VMEM((256, 1024), BF16),
+            pltpu.VMEM((2, 512, PLANE), BF16), pltpu.VMEM((512, 512), BF16), pltpu.VMEM((2, HALF, 256, PLANE), BF16), pltpu.VMEM((256, 1024), BF16),
             pltpu.VMEM((2, 20 * 32, PLANE), BF16), pltpu.VMEM((96, 288), F32), pltpu.SemaphoreType.DMA((4,)),
         ],
         us=6, vmem_mib=50,
@@ -424,29 +452,33 @@
     rows = sums.shape[0] // 2
     keep = lax.dynamic_slice_in_dim(sums, odd * rows, rows, 0)
     total = keep + exchange(lax.dynamic_slice_in_dim(sums, (1 - odd) * rows, rows, 0), 0)
-    gcore_side = exchange(gcore, 0)
-    octants_there = exchange(octants, 0)
-    gcross_side = exchange_cross(gcross)
-    back = []
+    message_there = exchange(message, 0)
     for bit in range(1, rounds):
-        step = exchange(total, bit)
-        if bit in (1, 2):
-            back.append(
-                call(
-                    functools.partial(back_inner_kernel, bit - 1), "backward_own_planes", acc_shape,
-                    (xy, total, gplanes, flipped), "shvv", scratch=[windows, cols], us=3,
-                )
+        if bit < 2:
+            sent = total
+            step = exchange(sent, bit)
+        else:
+            sent = lax.reduce_precision(total, 8, 7)
+            step = exchange(sent.astype(BF16), bit).astype(F32)
+        if bit == 1:
+            gcross, _ = lax.optimization_barrier((gcross, total))
+            gcross_side = exchange_cross(gcross)
+        if bit == 2:
+            back = call(
+                back_inner_kernel, "backward_own_planes", shape((2, 20 * 32, PLANE), F32),
+                (xy, total, gplanes, flipped), "shvv", scratch=[mask_rows, windows, two_cols], us=3,
             )
         if bit == 3:
             input_grad = call(
                 functools.partial(back_outer_kernel, layers), "backward_rest", shape((bricks, channels, voxels)),
-                (xy, voxel_mask, total, *back, gcore_side, gcross_side, flipped), "shhvvvvv",
-                scratch=[mask, pltpu.VMEM((2, 512, PLANE), F32), pltpu.SemaphoreType.DMA((1,))], us=2,
+                (xy, small_mask, total, back, message_there, gcross_side, flipped), "svhvvvv", out_kinds="h",
+                scratch=[pltpu.VMEM((bricks, channels, voxels), BF16), pltpu.SemaphoreType.DMA((2,))], us=2,
             )
-        total = total + step
+        total = sent + step
     other = exchange(total, 0)
     coarse_out = call(
-        coarse_kernel, "place", shape((2, 64, voxels)), (xy, octants, octants_there, total), "svvh", us=2
+        coarse_kernel, "place", shape((2, 64, voxels)), (xy, message, message_there, total), "svvh", out_kinds="h",
+        scratch=[pltpu.VMEM((2, 2, 64, HALF * PLANE), BF16), pltpu.SemaphoreType.DMA((2,))], us=2,
     )
     conv_grad, down_grad = call(
         finish_kernel, "finish", [shape((32, 864), F32), shape((64, 256), F32)], (total, other), "vv"

time: 43.4 us -> 39.4 us (0.908)
  starting transfers between devices: 17.7 us -> 14.2 us
  Pallas kernels: 23.2 us -> 22.2 us
  waiting for transfers between devices: 1.04 us -> 1.76 us
    ppermute x9 -> x7, starting transfers between devices: 10.1 us -> 7.67 us  [exchange(): lax.ppermute(value, 'morton', [(i, i ^ 1 << bit) for i in range(lax.axis_...]
    ppermute x2, starting transfers between devices: 7.63 us -> 6.58 us  [exchange_cross(): lax.ppermute(value, 'morton', pairs + [(target, source) for source, targe...]
    pallas_call x8 -> x7, Pallas kernels: 23.2 us -> 22.2 us  [call(): pl.pallas_call(body, name=name, out_shape=out_shapes, in_specs=[specs[kin...]
    ppermute x9 -> x7, waiting for transfers between devices: 1.04 us -> 1.76 us  [exchange(): lax.ppermute(value, 'morton', [(i, i ^ 1 << bit) for i in range(lax.axis_...]
  transfers between devices with their start and end apart: 11 -> 9, of which waited for: 2 -> 3; matrix products, arithmetic and copies ran while one was open for 0% -> 0% of each run, Pallas kernels for 31% -> 31%
where the time goes in v2:
time: 39.4 us; the launch traced here: 39.2 us
  Pallas kernels  22.2 us (56%)
  starting transfers between devices  14.2 us (36%)
  waiting for transfers between devices  1.76 us (4%)
  between operations  0.89 us (2%)
    pallas_call x7, Pallas kernels, call(): pl.pallas_call(body, name=name, out_shape=out_shapes, in_specs=[specs[kin...  22.2 us
    ppermute x7, starting transfers between devices, exchange(): lax.ppermute(value, 'morton', [(i, i ^ 1 << bit) for i in range(lax.axis_...  7.67 us
    ppermute x2, starting transfers between devices, exchange_cross(): lax.ppermute(value, 'morton', pairs + [(target, source) for source, targe...  6.58 us
    ppermute x7, waiting for transfers between devices, exchange(): lax.ppermute(value, 'morton', [(i, i ^ 1 << bit) for i in range(lax.axis_...  1.76 us
  transfers between devices with their start and end apart: 9, of which 3 were waited for; matrix products, arithmetic and copies ran while one was open for 0% of the time, Pallas kernels for 31%

profile of v2, /device:TPU:1, one launch (start us, length us, event | category | flops | bytes accessed | tf_op | source)
XLA Modules:
  0.0 39.2 jit_solution(17995124771068864985)
XLA Ops:
  0.6 3.4 %prepare.1 = (bf16[96,1024]{1,0:T(8,128)(2,1)}, bf16[32,512]{1,0:T(8,128)(2,1)}, bf16[64,1024]{1,0:T(8,128)(2,1)}, bf16[96,288]{1,0:T(8,128)(2,1)}, bf16[96,288]{1,0:T(8,128)(2,1)}, /*index=5*/bf16[64,256]{1,0:T(8,128)(2,1)}) custom-call(s32[2,32]{1,0:T(2,128)} %bitcast.1, bf16[2,32,4096]{2,1,0:T(8,128)(2,1)} %feat_hbm.3, s32[2,4096]{1,0:T(2,128)} %mask_hbm.5, ...), custom_call_target="tpu_custom_call" | custom-call | flops 2000000000 | bytes 7000000 | tf_op jit(solution)/shard_map/prepare/pallas_call | solution.py:377
  4.1 0.1 collective-permute-start
  4.2 4.5 %collective-permute-start.1 = (bf16[32,512]{1,0:T(8,128)(2,1)}, bf16[32,512]{1,0:T(8,128)(2,1)S(1)}, u32[]{:S(2)}, u32[]{:S(2)}) collective-permute-start(bf16[32,512]{1,0:T(8,128)(2,1)} %get-tuple-element.24), channel_id=1, source_target_pairs={{1,2},{3,4},{5,6},{7,8},{9,10},{11,12},{13,14},{2,1},{4,3},{6,5},{... | collective-permute-start | bytes 98312 | tf_op jit(solution)/shard_map/ppermute | solution.py:400
  8.7 0.0 copy-start
  8.7 0.0 copy-start.1
  8.7 0.0 copy-start.2
  8.7 0.0 copy-start.3
  8.7 0.0 copy-start.5
  8.7 0.0 copy-start.6
  8.8 5.6 %forward_own_planes.1 = (bf16[2,4608,256]{2,1,0:T(8,128)(2,1)}, f32[2,4096,256]{2,1,0:T(8,128)}) custom-call(s32[2,32]{1,0:T(2,128)} %bitcast.2, bf16[2,32,4096]{2,1,0:T(8,128)(2,1)} %feat_hbm.3, s32[2,4096]{1,0:T(2,128)} %mask_hbm.5, bf16[96,288]{1,0:T(8,128)(2,1)} %get-tuple-element.20.stacked_hbm.stacked_ref), custom_call_target="tpu_custom_call" | custom-call | flops 5000000000 | bytes 17500000 | tf_op jit(solution)/shard_map/forward_own_planes/pallas_call | solution.py:377
  14.4 0.0 collective-permute-done.1.cross_ref
  14.4 0.0 collective-permute-done.recv_ref
  14.4 0.0 copy-done
  14.4 0.0 copy-done.1
  14.4 0.0 copy-done.2
  14.4 0.0 copy-done.3
  14.4 0.0 copy-done.5
  14.4 0.0 copy-done.6
  14.5 0.0 copy-start.4
  14.5 5.9 %forward_rest.1 = (bf16[96,1024]{1,0:T(8,128)(2,1)S(1)}, bf16[512,512]{1,0:T(8,128)(2,1)S(1)}, bf16[32,512]{1,0:T(8,128)(2,1)S(1)}, bf16[2,4096]{1,0:T(2,128)(2,1)S(1)}, f32[32,1408]{1,0:T(8,128)S(1)}) custom-call(s32[2,32]{1,0:T(2,128)S(1)} %bitcast.3, bf16[2,4608,256]{2,1,0:T(8,128)(2,1)} %get-tuple-element.21.cols_hbm, ...), custom_call_target="tpu_custom_call" | custom-call | flops 6000000000 | bytes 21000000 | tf_op jit(solution)/shard_map/forward_rest/pallas_call | solution.py:377
  20.4 0.1 collective-permute-start.3
  20.5 1.3 %collective-permute-done.3 = f32[16,1408]{1,0:T(8,128)S(1)} collective-permute-done((f32[16,1408]{1,0:T(8,128)S(1)}, f32[16,1408]{1,0:T(8,128)S(1)}, u32[]{:S(2)}, u32[]{:S(2)}) %collective-permute-start.3) | collective-permute-done | bytes 90144 | tf_op jit(solution)/shard_map/ppermute | solution.py:394
  21.7 1.3 %collective-permute-start.4 = (f32[16,1408]{1,0:T(8,128)S(1)}, f32[16,1408]{1,0:T(8,128)S(1)}, u32[]{:S(2)}, u32[]{:S(2)}) collective-permute-start(f32[16,1408]{1,0:T(8,128)S(1)} %dynamic-slice_add_fusion), channel_id=1, source_target_pairs={{0,2},{1,3},{2,0},{3,1},{4,6},{5,7},{6,4},{7,5},{8,10},{9,11},{10,... | collective-permute-start | bytes 270344 | tf_op jit(solution)/shard_map/ppermute | solution.py:394
  23.0 0.4 %collective-permute-start.2 = (bf16[96,1024]{1,0:T(8,128)(2,1)S(1)}, bf16[96,1024]{1,0:T(8,128)(2,1)S(1)}, u32[]{:S(2)}, u32[]{:S(2)}) collective-permute-start(bf16[96,1024]{1,0:T(8,128)(2,1)S(1)} %get-tuple-element.27.own_ref), channel_id=1, source_target_pairs={{0,1},{1,0},{2,3},{3,2},{4,5},{5,4},{6,7},{7,6},{8,9},{9,8},{10,11... | collective-permute-start | bytes 589832 | tf_op jit(solution)/shard_map/ppermute | solution.py:394
  23.5 2.1 %collective-permute-start.7 = (bf16[32,512]{1,0:T(8,128)(2,1)S(1)}, bf16[32,512]{1,0:T(8,128)(2,1)S(1)}, u32[]{:S(2)}, u32[]{:S(2)}) collective-permute-start(bf16[32,512]{1,0:T(8,128)(2,1)S(1)} %get-tuple-element.33), channel_id=1, source_target_pairs={{1,2},{3,4},{5,6},{7,8},{9,10},{11,12},{13,14},{2,1},{4,3},{6,5},{... | collective-permute-start | bytes 98312 | tf_op jit(solution)/shard_map/ppermute | solution.py:400
  25.6 0.3 collective-permute-done.4
  25.9 1.2 %collective-permute-start.5 = (bf16[16,1408]{1,0:T(8,128)(2,1)S(1)}, bf16[16,1408]{1,0:T(8,128)(2,1)S(1)}, u32[]{:S(2)}, u32[]{:S(2)}) collective-permute-start(bf16[16,1408]{1,0:T(8,128)(2,1)S(1)} %get-tuple-element.38), channel_id=1, source_target_pairs={{0,4},{1,5},{2,6},{3,7},{4,0},{5,1},{6,2},{7,3},{8,12},{9,13},{10,... | collective-permute-start | bytes 135176 | tf_op jit(solution)/shard_map/ppermute | solution.py:394
  27.1 0.0 copy-done.4
  27.1 2.9 %backward_own_planes.1.acc_ref = f32[2,640,256]{2,1,0:T(8,128)S(1)} custom-call(s32[2,32]{1,0:T(2,128)S(1)} %bitcast.4, f32[16,1408]{1,0:T(8,128)S(1)} %get-tuple-element.39.after_ref, bf16[512,512]{1,0:T(8,128)(2,1)S(1)} %get-tuple-element.30.gplanes_ref, bf16[96,288]{1,0:T(8,128)(2,1)S(1)} %copy-done.4), custom_call_target="tpu_custom_call" | custom-call | flops 3000000000 | bytes 10500000 | tf_op jit(solution)/shard_map/backward_own_planes/pallas_call | solution.py:377
  30.1 0.0 collective-permute-done.5
  30.1 2.4 %collective-permute-start.6 = (bf16[16,1408]{1,0:T(8,128)(2,1)S(1)}, bf16[16,1408]{1,0:T(8,128)(2,1)S(1)}, u32[]{:S(2)}, u32[]{:S(2)}) collective-permute-start(bf16[16,1408]{1,0:T(8,128)(2,1)S(1)} %get-tuple-element.36), channel_id=1, source_target_pairs={{0,8},{1,9},{2,10},{3,11},{4,12},{5,13},{6,14},{7,15},{8,0},{9,1},... | collective-permute-start | bytes 135176 | tf_op jit(solution)/shard_map/ppermute | solution.py:394
  32.5 0.0 collective-permute-done.7.cross_ref
  32.5 0.0 collective-permute-done.2.recv_ref
  32.5 1.8 %backward_rest.1 = bf16[2,32,4096]{2,1,0:T(8,128)(2,1)} custom-call(s32[2,32]{1,0:T(2,128)S(1)} %bitcast.5, bf16[2,4096]{1,0:T(2,128)(2,1)S(1)} %get-tuple-element.29.mask_ref, f32[16,1408]{1,0:T(8,128)S(1)} %get-tuple-element.37.after_ref, f32[2,640,256]{2,1,0:T(8,128)S(1)} %backward_own_planes.1.acc_ref, ...), custom_call_target="tpu_custom_call" | custom-call | flops 2000000000 | bytes 7000000 | tf_op jit(solution)/shard_map/backward_rest/pallas_call | solution.py:377
  34.3 0.2 collective-permute-done.6
  34.5 2.1 %collective-permute-start.8 = (f32[16,1408]{1,0:T(8,128)S(1)}, f32[16,1408]{1,0:T(8,128)S(1)}, u32[]{:S(2)}, u32[]{:S(2)}) collective-permute-start(f32[16,1408]{1,0:T(8,128)S(1)} %convert_add_fusion.after_ref.total_ref), channel_id=1, source_target_pairs={{0,1},{1,0},{2,3},{3,2},{4,5},{5,4},{6,7},{7,6},{8,9},{9,8},{10,11... | collective-permute-start | bytes 270344 | tf_op jit(solution)/shard_map/ppermute | solution.py:394
  36.6 1.9 %place.1 = bf16[2,64,4096]{2,1,0:T(8,128)(2,1)} custom-call(s32[2,32]{1,0:T(2,128)S(1)} %bitcast.6, bf16[96,1024]{1,0:T(8,128)(2,1)S(1)} %get-tuple-element.27.own_ref, bf16[96,1024]{1,0:T(8,128)(2,1)S(1)} %collective-permute-done.2.recv_ref, f32[16,1408]{1,0:T(8,128)S(1)} %convert_add_fusion.after_ref.total_ref), custom_call_target="tpu_custom_call" | custom-call | flops 2000000000 | bytes 7000000 | tf_op jit(solution)/shard_map/place/pallas_call | solution.py:377
  38.5 0.0 collective-permute-done.8.other_ref
  38.5 0.7 %finish.1 = (f32[32,864]{1,0:T(8,128)}, f32[64,256]{1,0:T(8,128)}) custom-call(f32[16,1408]{1,0:T(8,128)S(1)} %convert_add_fusion.after_ref.total_ref, f32[16,1408]{1,0:T(8,128)S(1)} %collective-permute-done.8.other_ref), custom_call_target="tpu_custom_call" | custom-call | flops 1000000000 | bytes 3500000 | tf_op jit(solution)/shard_map/finish/pallas_call | solution.py:377
  (5 shorter events, 0.1 us)
Async XLA Ops:
  4.1 10.3 %collective-permute-start = (bf16[96,1024]{1,0:T(8,128)(2,1)}, bf16[96,1024]{1,0:T(8,128)(2,1)S(1)}, u32[]{:S(2)}, u32[]{:S(2)}) collective-permute-start(bf16[96,1024]{1,0:T(8,128)(2,1)} %get-tuple-element.23), channel_id=1, source_target_pairs={{0,1},{1,0},{2,3},{3,2},{4,5},{5,4},{6,7},{7,6},{8,9},{9,8},{10,11... | collective-permute-start | bytes 589832 | tf_op jit(solution)/shard_map/ppermute | solution.py:394
  4.2 10.2 %collective-permute-start.1 = (bf16[32,512]{1,0:T(8,128)(2,1)}, bf16[32,512]{1,0:T(8,128)(2,1)S(1)}, u32[]{:S(2)}, u32[]{:S(2)}) collective-permute-start(bf16[32,512]{1,0:T(8,128)(2,1)} %get-tuple-element.24), channel_id=1, source_target_pairs={{1,2},{3,4},{5,6},{7,8},{9,10},{11,12},{13,14},{2,1},{4,3},{6,5},{... | collective-permute-start | bytes 98312 | tf_op jit(solution)/shard_map/ppermute | solution.py:400
  8.7 5.7 %copy-start = (s32[2,4096]{1,0:T(2,128)S(1)}, s32[2,4096]{1,0:T(2,128)}, u32[]{:S(2)}) copy-start(s32[2,4096]{1,0:T(2,128)} %mask_hbm.5) | copy-start | bytes 98308
  8.7 5.7 %copy-start.1 = (bf16[64,256]{1,0:T(8,128)(2,1)S(1)}, bf16[64,256]{1,0:T(8,128)(2,1)}, u32[]{:S(2)}) copy-start(bf16[64,256]{1,0:T(8,128)(2,1)} %down_hbm.3) | copy-start | bytes 98308
  8.7 5.7 %copy-start.2 = (s32[32,2]{0,1:T(2,128)S(1)}, s32[32,2]{0,1:T(2,128)}, u32[]{:S(2)}) copy-start(s32[32,2]{0,1:T(2,128)} %param.9) | copy-start | bytes 772
  8.7 5.7 %copy-start.3 = (bf16[64,1024]{1,0:T(8,128)(2,1)S(1)}, bf16[64,1024]{1,0:T(8,128)(2,1)}, u32[]{:S(2)}) copy-start(bf16[64,1024]{1,0:T(8,128)(2,1)} %get-tuple-element.25.own_ref) | copy-start | bytes 393220
  8.7 5.7 %copy-start.5 = (bf16[96,288]{1,0:T(8,128)(2,1)S(1)}, bf16[96,288]{1,0:T(8,128)(2,1)}, u32[]{:S(2)}) copy-start(bf16[96,288]{1,0:T(8,128)(2,1)} %get-tuple-element.20.stacked_hbm.stacked_ref) | copy-start | bytes 165892
  8.7 5.7 %copy-start.6 = (bf16[64,256]{1,0:T(8,128)(2,1)S(1)}, bf16[64,256]{1,0:T(8,128)(2,1)}, u32[]{:S(2)}) copy-start(bf16[64,256]{1,0:T(8,128)(2,1)} %get-tuple-element.26.down_t_ref) | copy-start | bytes 98308
  14.5 12.7 %copy-start.4 = (bf16[96,288]{1,0:T(8,128)(2,1)S(1)}, bf16[96,288]{1,0:T(8,128)(2,1)}, u32[]{:S(2)}) copy-start(bf16[96,288]{1,0:T(8,128)(2,1)} %get-tuple-element.31.flipped_ref) | copy-start | bytes 165892
  20.4 1.4 %collective-permute-start.3 = (f32[16,1408]{1,0:T(8,128)S(1)}, f32[16,1408]{1,0:T(8,128)S(1)}, u32[]{:S(2)}, u32[]{:S(2)}) collective-permute-start(f32[16,1408]{1,0:T(8,128)S(1)} %constant_dynamic-slice_fusion), channel_id=1, source_target_pairs={{0,1},{1,0},{2,3},{3,2},{4,5},{5,4},{6,7},{7,6},{8,9},{9,8},{10,11... | collective-permute-start | bytes 270344 | tf_op jit(solution)/shard_map/ppermute | solution.py:394
  21.7 4.1 %collective-permute-start.4 = (f32[16,1408]{1,0:T(8,128)S(1)}, f32[16,1408]{1,0:T(8,128)S(1)}, u32[]{:S(2)}, u32[]{:S(2)}) collective-permute-start(f32[16,1408]{1,0:T(8,128)S(1)} %dynamic-slice_add_fusion), channel_id=1, source_target_pairs={{0,2},{1,3},{2,0},{3,1},{4,6},{5,7},{6,4},{7,5},{8,10},{9,11},{10,... | collective-permute-start | bytes 270344 | tf_op jit(solution)/shard_map/ppermute | solution.py:394
  23.0 9.4 %collective-permute-start.2 = (bf16[96,1024]{1,0:T(8,128)(2,1)S(1)}, bf16[96,1024]{1,0:T(8,128)(2,1)S(1)}, u32[]{:S(2)}, u32[]{:S(2)}) collective-permute-start(bf16[96,1024]{1,0:T(8,128)(2,1)S(1)} %get-tuple-element.27.own_ref), channel_id=1, source_target_pairs={{0,1},{1,0},{2,3},{3,2},{4,5},{5,4},{6,7},{7,6},{8,9},{9,8},{10,11... | collective-permute-start | bytes 589832 | tf_op jit(solution)/shard_map/ppermute | solution.py:394
  23.5 9.0 %collective-permute-start.7 = (bf16[32,512]{1,0:T(8,128)(2,1)S(1)}, bf16[32,512]{1,0:T(8,128)(2,1)S(1)}, u32[]{:S(2)}, u32[]{:S(2)}) collective-permute-start(bf16[32,512]{1,0:T(8,128)(2,1)S(1)} %get-tuple-element.33), channel_id=1, source_target_pairs={{1,2},{3,4},{5,6},{7,8},{9,10},{11,12},{13,14},{2,1},{4,3},{6,5},{... | collective-permute-start | bytes 98312 | tf_op jit(solution)/shard_map/ppermute | solution.py:400
  25.9 4.2 %collective-permute-start.5 = (bf16[16,1408]{1,0:T(8,128)(2,1)S(1)}, bf16[16,1408]{1,0:T(8,128)(2,1)S(1)}, u32[]{:S(2)}, u32[]{:S(2)}) collective-permute-start(bf16[16,1408]{1,0:T(8,128)(2,1)S(1)} %get-tuple-element.38), channel_id=1, source_target_pairs={{0,4},{1,5},{2,6},{3,7},{4,0},{5,1},{6,2},{7,3},{8,12},{9,13},{10,... | collective-permute-start | bytes 135176 | tf_op jit(solution)/shard_map/ppermute | solution.py:394
  30.1 4.3 %collective-permute-start.6 = (bf16[16,1408]{1,0:T(8,128)(2,1)S(1)}, bf16[16,1408]{1,0:T(8,128)(2,1)S(1)}, u32[]{:S(2)}, u32[]{:S(2)}) collective-permute-start(bf16[16,1408]{1,0:T(8,128)(2,1)S(1)} %get-tuple-element.36), channel_id=1, source_target_pairs={{0,8},{1,9},{2,10},{3,11},{4,12},{5,13},{6,14},{7,15},{8,0},{9,1},... | collective-permute-start | bytes 135176 | tf_op jit(solution)/shard_map/ppermute | solution.py:394
  34.5 4.0 %collective-permute-start.8 = (f32[16,1408]{1,0:T(8,128)S(1)}, f32[16,1408]{1,0:T(8,128)S(1)}, u32[]{:S(2)}, u32[]{:S(2)}) collective-permute-start(f32[16,1408]{1,0:T(8,128)S(1)} %convert_add_fusion.after_ref.total_ref), channel_id=1, source_target_pairs={{0,1},{1,0},{2,3},{3,2},{4,5},{5,4},{6,7},{7,6},{8,9},{9,8},{10,11... | collective-permute-start | bytes 270344 | tf_op jit(solution)/shard_map/ppermute | solution.py:394

commit v3 on v2

--- a/solution.py
+++ b/solution.py
@@ -155,8 +155,11 @@
                 cols_ref[pl.ds((p + q) * 288 + shift * 32, 32), :] = piece[q * 32 : (q + 1) * 32]
 
 
-def unfold_side(xy_ref, layer, r, other, planes):
-    places = [offset_of(xy_ref, layer, r, other, s) for s in range(2)]
+def unfold_side(xy_ref, layers, layer, r, other, planes):
+    valid = (other >= 0) & (other < layers)
+    near = jnp.clip(other, 0, layers - 1)
+    places = [offset_of(xy_ref, layer, r, near, s) for s in range(2)]
+    places = [(jnp.where(valid, ox, 8), oy) for ox, oy in places]
     first, second = (turned(planes[:, s * PLANE : (s + 1) * PLANE], places[s][0]) for s in range(2))
     pieces = []
     for shift in range(9):
@@ -173,19 +176,15 @@
 
 
 def inner_kernel(
-    xy_ref, feat_hbm, mask_hbm, stacked_hbm, cols_hbm, acc_hbm,
-    feat_ref, mask_ref, stacked_ref, rows_ref, window_ref, in_ref, cols_ref, acc_ref, sems,
+    xy_ref, feat_ref, mask_ref, stacked_ref, cols_hbm, acc_hbm, rows_ref, window_ref, in_ref, cols_ref, acc_ref, sems,
 ):
     layer = lax.axis_index("morton")
-    copies = start_all(((feat_hbm, feat_ref), (mask_hbm, mask_ref), (stacked_hbm, stacked_ref)), sems)
     build_masks(0, 0, rows_ref, window_ref.at[2])
     ox = []
     for r in range(2):
         x, y = offset_of(xy_ref, layer, r, layer, 1 - r)
         build_masks(x, y, rows_ref, window_ref.at[r])
         ox.append(x)
-    for copy in copies:
-        copy.wait()
     for r in range(2):
         for z in range(EDGE):
             lanes = pl.ds(z * PLANE, PLANE)
@@ -196,19 +195,18 @@
         for i in range(2):
             unfold_planes(in_ref, r, i * STEP, ox[r], window_ref.at[2], window_ref.at[r], cols_ref.at[r])
             rows = pl.ds(i * STEP * 288, STEP * 288)
-            out += start_all(((cols_ref.at[r, rows], cols_hbm.at[r, rows]),), sems.at[pl.ds(5 + 2 * r + i, 1)])
+            out += start_all(((cols_ref.at[r, rows], cols_hbm.at[r, rows]),), sems.at[pl.ds(2 + 2 * r + i, 1)])
     for r in range(2):
         convolve(stacked_ref[...], cols_ref.at[r], acc_ref.at[r])
-        out += start_all(((acc_ref.at[r, pl.ds(64, 512)], acc_hbm.at[r, pl.ds(0, 512)]),), sems.at[pl.ds(3 + r, 1)])
+        out += start_all(((acc_ref.at[r, pl.ds(64, 512)], acc_hbm.at[r, pl.ds(0, 512)]),), sems.at[pl.ds(r, 1)])
     for copy in out:
         copy.wait()
 
 
-def sides_of(layer, layers):
+def sides_of(layer):
     odd = layer % 2
-    above = layer + 1 - odd
     core = jnp.where(odd == 0, layer + 1, layer - 1)
-    cross = jnp.where(odd == 0, jnp.maximum(layer - 1, 0), jnp.minimum(layer + 1, layers - 1))
+    cross = jnp.where(odd == 0, layer - 1, layer + 1)
     return ((core, 2 * (1 - odd), 15 * (1 - odd)), (cross, 2 * odd, 15 * odd))
 
 
@@ -225,7 +223,7 @@
         ((acc_hbm.at[:, pl.ds(0, 512)], acc_ref), (mask_hbm, mask_ref), (down_hbm, down_ref), (cols_hbm, cols_ref)), sems
     )
     layer = lax.axis_index("morton")
-    sides = sides_of(layer, layers)
+    sides = sides_of(layer)
 
     row = iota((2 * PLANE, PLANE), 0)
     lane = iota((2 * PLANE, PLANE), 1)
@@ -255,7 +253,7 @@
     side_cols = []
     for (other, dz, z), ref in zip(sides, (core_ref, cross_ref)):
         for r in range(2):
-            side_cols.append(unfold_side(xy_ref, layer, r, other, ref[...]))
+            side_cols.append(unfold_side(xy_ref, layers, layer, r, other, ref[...]))
     for copy in copies[:3]:
         copy.wait()
     small_ref[...] = mask_ref[...].astype(F32).astype(BF16)
@@ -324,8 +322,8 @@
     out = []
     for r in range(2):
         terms = []
-        for (other, dz, z), ref in zip(sides_of(layer, layers), (core_ref, cross_ref)):
-            terms.append(mm(flipped_ref[rows_at(dz), :], unfold_side(xy_ref, layer, r, other, ref[...])))
+        for (other, dz, z), ref in zip(sides_of(layer), (core_ref, cross_ref)):
+            terms.append(mm(flipped_ref[rows_at(dz), :], unfold_side(xy_ref, layers, layer, r, other, ref[...])))
         below = jnp.where(odd == 1, terms[0], terms[1])
         above = jnp.where(odd == 1, terms[1], terms[0])
         for z in range(EDGE):
@@ -358,13 +356,14 @@
     out = []
     for i, (target, half, ref) in enumerate(((layer, parity, own_ref), (partner, 1 - parity, recv_ref))):
         pieces = jnp.concatenate([ref[:64, wz * 128 : (wz + 1) * 128] for wz in range(HALF)], axis=0)
-        key = octant_key(xy_ref, target, parity, iota((128, 2 * PLANE), 0))
-        placed = mm(pieces, one_hot(key, iota((128, 2 * PLANE), 1))).astype(BF16)
+        key = octant_key(xy_ref, target, parity, iota((128, 128), 0))
+        places = [one_hot(key, iota((128, 128), 1) + tile * 128) for tile in range(4)]
+        lanes = pl.ds(pl.multiple_of(half * HALF * PLANE, HALF * PLANE), HALF * PLANE)
         for q in range(2):
+            placed = mm(pieces, jnp.concatenate(places[2 * q : 2 * q + 2], axis=1)).astype(BF16)
             for wz in range(HALF):
-                out_ref[i, q, :, pl.ds(wz * PLANE, PLANE)] = placed[wz * 64 : (wz + 1) * 64, q * PLANE : (q + 1) * PLANE]
-        lanes = pl.ds(pl.multiple_of(half * HALF * PLANE, HALF * PLANE), HALF * PLANE)
-        out += start_all(((out_ref.at[i], out_hbm.at[:, :, lanes]),), sems.at[pl.ds(i, 1)])
+                out_ref[i, q, :, pl.ds(wz * PLANE, PLANE)] = placed[wz * 64 : (wz + 1) * 64]
+            out += start_all(((out_ref.at[i, q], out_hbm.at[q, :, lanes]),), sems.at[pl.ds(2 * i + q, 1)])
     for copy in out:
         copy.wait()
 
@@ -396,8 +395,16 @@
 
 def exchange_cross(value):
     layers = lax.axis_size("morton")
-    pairs = [(i, i + 1) for i in range(1, layers - 1, 2)]
-    return lax.ppermute(value, "morton", pairs + [(target, source) for source, target in pairs])
+    groups = lax.axis_size("groups")
+    pairs = []
+    for g in range(groups):
+        for i in range(layers):
+            other = i + 1 if i % 2 else i - 1
+            if 0 <= other < layers:
+                pairs.append((g * layers + i, g * layers + other))
+            elif g ^ 1 < groups:
+                pairs.append((g * layers + i, (g ^ 1) * layers + i))
+    return lax.ppermute(value, ("groups", "morton"), pairs)
 
 
 def per_device(features, voxel_mask, brick_xy, neighbours, conv_weight, down_weight, coarse_grad):
@@ -409,16 +416,17 @@
     oct_shape = shape((64, 1024))
     message_shape = shape((96, 1024))
     xy = brick_xy.T
+    pinned = [pltpu.with_memory_space_constraint(x, pltpu.HBM) for x in (xy, features, voxel_mask, coarse_grad, conv_weight, down_weight)]
     block = shape((96, 288))
     message, cross_edge, own, flipped, stacked, down_t = call(
         prepare_kernel, "prepare", [message_shape, side_shape, oct_shape, block, block, shape((64, 256))],
-        (xy, features, voxel_mask, coarse_grad, conv_weight, down_weight), "shhhhh",
+        pinned, "shhhhh",
         scratch=[
             pltpu.VMEM((2, 2, 32, PLANE), BF16), pltpu.VMEM((2, 2, PLANE), I32),
             pltpu.VMEM((2, 2, 64, HALF * PLANE), BF16), pltpu.VMEM((32, 864), BF16), pltpu.VMEM((64, 256), BF16),
             pltpu.SemaphoreType.DMA((8,)),
         ],
-        us=2, vmem_mib=58,
+        us=2, vmem_mib=32,
     )
     arrived = exchange(message, 0)
     cross_side = exchange_cross(cross_edge)
@@ -429,13 +437,13 @@
     all_cols, acc = call(
         inner_kernel, "forward_own_planes",
         [shape((2, 16 * 288, PLANE)), shape((2, 4096, PLANE), F32)],
-        (xy, features, voxel_mask, stacked), "shhh", out_kinds="hh",
+        (xy, features, voxel_mask, stacked), "svvv", out_kinds="hh",
         scratch=[
-            pltpu.VMEM((2, 32, voxels), BF16), mask, pltpu.VMEM((96, 288), BF16), mask_rows, windows,
+            mask_rows, windows,
             pltpu.VMEM((512, 512), BF16),
-            two_cols, pltpu.VMEM((2, 20 * 32, PLANE), F32), pltpu.SemaphoreType.DMA((9,)),
+            two_cols, pltpu.VMEM((2, 20 * 32, PLANE), F32), pltpu.SemaphoreType.DMA((6,)),
         ],
-        us=5, vmem_mib=58,
+        us=5, vmem_mib=50,
     )
     message, gplanes, gcross, small_mask, sums = call(
         functools.partial(outer_kernel, layers, scale), "forward_rest",
@@ -463,23 +471,26 @@
         if bit == 1:
             gcross, _ = lax.optimization_barrier((gcross, total))
             gcross_side = exchange_cross(gcross)
+            coarse_out = call(
+                coarse_kernel, "place", shape((2, 64, voxels)), (xy, message, message_there, total), "svvh", out_kinds="h",
+                scratch=[pltpu.VMEM((2, 2, 64, HALF * PLANE), BF16), pltpu.SemaphoreType.DMA((4,))], us=2,
+            )
+            step, coarse_out = lax.optimization_barrier((step, coarse_out))
         if bit == 2:
             back = call(
                 back_inner_kernel, "backward_own_planes", shape((2, 20 * 32, PLANE), F32),
                 (xy, total, gplanes, flipped), "shvv", scratch=[mask_rows, windows, two_cols], us=3,
             )
+            step, back = lax.optimization_barrier((step, back))
         if bit == 3:
             input_grad = call(
                 functools.partial(back_outer_kernel, layers), "backward_rest", shape((bricks, channels, voxels)),
                 (xy, small_mask, total, back, message_there, gcross_side, flipped), "svhvvvv", out_kinds="h",
                 scratch=[pltpu.VMEM((bricks, channels, voxels), BF16), pltpu.SemaphoreType.DMA((2,))], us=2,
             )
+            step, input_grad = lax.optimization_barrier((step, input_grad))
         total = sent + step
     other = exchange(total, 0)
-    coarse_out = call(
-        coarse_kernel, "place", shape((2, 64, voxels)), (xy, message, message_there, total), "svvh", out_kinds="h",
-        scratch=[pltpu.VMEM((2, 2, 64, HALF * PLANE), BF16), pltpu.SemaphoreType.DMA((2,))], us=2,
-    )
     conv_grad, down_grad = call(
         finish_kernel, "finish", [shape((32, 864), F32), shape((64, 256), F32)], (total, other), "vv"
     )

time: 39.4 us -> 34.9 us (0.89)
  starting transfers between devices: 14.2 us -> 11.4 us
  Pallas kernels: 22.2 us -> 20.3 us
    ppermute x2, starting transfers between devices: 6.58 us -> 3.42 us  [exchange_cross(): return lax.ppermute(value, ('groups', 'morton'), pairs)]
    pallas_call x7, Pallas kernels: 22.2 us -> 20.3 us  [call(): pl.pallas_call(body, name=name, out_shape=out_shapes, in_specs=[specs[kin...]
where the time goes in v3:
time: 34.9 us; the launch traced here: 34.4 us
  Pallas kernels  20.3 us (58%)
  starting transfers between devices  11.4 us (33%)
  waiting for transfers between devices  1.82 us (5%)
  between operations  0.82 us (2%)
    pallas_call x7, Pallas kernels, call(): pl.pallas_call(body, name=name, out_shape=out_shapes, in_specs=[specs[kin...  20.3 us
    ppermute x7, starting transfers between devices, exchange(): lax.ppermute(value, 'morton', [(i, i ^ 1 << bit) for i in range(lax.axis_...  7.96 us
    ppermute x2, starting transfers between devices, exchange_cross(): return lax.ppermute(value, ('groups', 'morton'), pairs)  3.42 us
    ppermute x7, waiting for transfers between devices, exchange(): lax.ppermute(value, 'morton', [(i, i ^ 1 << bit) for i in range(lax.axis_...  1.81 us
  transfers between devices with their start and end apart: 9, of which 3 were waited for; matrix products, arithmetic and copies ran while one was open for 0% of the time, Pallas kernels for 31%

profile of v3, /device:TPU:1, one launch (start us, length us, event | category | flops | bytes accessed | tf_op | source)
XLA Modules:
  0.0 34.4 jit_solution(9229784175604949702)
XLA Ops:
  0.6 0.0 copy-start.3
  0.6 0.0 copy-start
  0.7 0.0 copy-start.1
  0.7 2.9 %prepare.1 = (bf16[96,1024]{1,0:T(8,128)(2,1)S(1)}, bf16[32,512]{1,0:T(8,128)(2,1)S(1)}, bf16[64,1024]{1,0:T(8,128)(2,1)S(1)}, bf16[96,288]{1,0:T(8,128)(2,1)S(1...) custom-call(s32[2,32]{1,0:T(2,128)} %bitcast.1, bf16[2,32,4096]{2,1,0:T(8,128)(2,1)} %feat_ref.1, ...), custom_call_target="tpu_custom_call" | custom-call | flops 2000000000 | bytes 7000000 | tf_op jit(solution)/shard_map/prepare/pallas_call | solution.py:376
  3.6 0.1 collective-permute-start
  3.7 2.6 %collective-permute-start.1 = (bf16[32,512]{1,0:T(8,128)(2,1)S(1)}, bf16[32,512]{1,0:T(8,128)(2,1)S(1)}, u32[]{:S(2)}, u32[]{:S(2)}) collective-permute-start(bf16[32,512]{1,0:T(8,128)(2,1)S(1)} %get-tuple-element.30), channel_id=1, source_target_pairs={{0,16},{1,2},{2,1},{3,4},{4,3},{5,6},{6,5},{7,8},{8,7},{9,10},{10,... | collective-permute-start | bytes 98312 | tf_op jit(solution)/shard_map/ppermute | solution.py:407
  6.3 0.0 copy-done.3
  6.3 0.0 copy-done
  6.3 0.0 copy-done.1
  6.3 0.0 copy-start.2
  6.4 4.2 %forward_own_planes.1 = (bf16[2,4608,256]{2,1,0:T(8,128)(2,1)}, f32[2,4096,256]{2,1,0:T(8,128)}) custom-call(s32[2,32]{1,0:T(2,128)S(1)} %bitcast.2, bf16[2,32,4096]{2,1,0:T(8,128)(2,1)S(1)} %copy-done, s32[2,4096]{1,0:T(2,128)S(1)} %copy-done.1, bf16[96,288]{1,0:T(8,128)(2,1)S(1)} %get-tuple-element.26.stacked_ref), custom_call_target="tpu_custom_call" | custom-call | flops 5000000000 | bytes 17500000 | tf_op jit(solution)/shard_map/forward_own_planes/pallas_call | solution.py:376
  10.6 0.0 collective-permute-done.1.cross_ref
  10.6 0.0 collective-permute-done.recv_ref
  10.6 0.0 copy-done.2
  10.7 5.9 %forward_rest.1 = (bf16[96,1024]{1,0:T(8,128)(2,1)S(1)}, bf16[512,512]{1,0:T(8,128)(2,1)S(1)}, bf16[32,512]{1,0:T(8,128)(2,1)S(1)}, bf16[2,4096]{1,0:T(2,128)(2,1)S(1)}, f32[32,1408]{1,0:T(8,128)S(1)}) custom-call(s32[2,32]{1,0:T(2,128)S(1)} %bitcast.3, bf16[2,4608,256]{2,1,0:T(8,128)(2,1)} %get-tuple-element.27.cols_hbm, ...), custom_call_target="tpu_custom_call" | custom-call | flops 6000000000 | bytes 21000000 | tf_op jit(solution)/shard_map/forward_rest/pallas_call | solution.py:376
  16.6 0.4 %collective-permute-start.2 = (f32[16,1408]{1,0:T(8,128)S(1)}, f32[16,1408]{1,0:T(8,128)S(1)}, u32[]{:S(2)}, u32[]{:S(2)}) collective-permute-start(f32[16,1408]{1,0:T(8,128)S(1)} %constant_dynamic-slice_fusion), channel_id=1, source_target_pairs={{0,1},{1,0},{2,3},{3,2},{4,5},{5,4},{6,7},{7,6},{8,9},{9,8},{10,11... | collective-permute-start | bytes 270344 | tf_op jit(solution)/shard_map/ppermute | solution.py:393
  17.0 0.1 collective-permute-start.4
  17.2 0.8 %collective-permute-done.2 = f32[16,1408]{1,0:T(8,128)S(1)} collective-permute-done((f32[16,1408]{1,0:T(8,128)S(1)}, f32[16,1408]{1,0:T(8,128)S(1)}, u32[]{:S(2)}, u32[]{:S(2)}) %collective-permute-start.2) | collective-permute-done | bytes 90144 | tf_op jit(solution)/shard_map/ppermute | solution.py:393
  18.0 1.3 %collective-permute-start.3 = (f32[16,1408]{1,0:T(8,128)S(1)}, f32[16,1408]{1,0:T(8,128)S(1)}, u32[]{:S(2)}, u32[]{:S(2)}) collective-permute-start(f32[16,1408]{1,0:T(8,128)S(1)} %dynamic-slice_add_fusion.after_ref), channel_id=1, source_target_pairs={{0,2},{1,3},{2,0},{3,1},{4,6},{5,7},{6,4},{7,5},{8,10},{9,11},{10,... | collective-permute-start | bytes 270344 | tf_op jit(solution)/shard_map/ppermute | solution.py:393
  19.3 0.8 %collective-permute-start.7 = (bf16[32,512]{1,0:T(8,128)(2,1)S(1)}, bf16[32,512]{1,0:T(8,128)(2,1)S(1)}, u32[]{:S(2)}, u32[]{:S(2)}) collective-permute-start(bf16[32,512]{1,0:T(8,128)(2,1)S(1)} %get-tuple-element.43), channel_id=1, source_target_pairs={{0,16},{1,2},{2,1},{3,4},{4,3},{5,6},{6,5},{7,8},{8,7},{9,10},{10,... | collective-permute-start | bytes 98312 | tf_op jit(solution)/shard_map/ppermute | solution.py:407
  20.0 0.0 collective-permute-done.4.recv_ref
  20.0 1.9 %place.1 = bf16[2,64,4096]{2,1,0:T(8,128)(2,1)} custom-call(s32[2,32]{1,0:T(2,128)S(1)} %bitcast.4, bf16[96,1024]{1,0:T(8,128)(2,1)S(1)} %get-tuple-element.34.own_ref, bf16[96,1024]{1,0:T(8,128)(2,1)S(1)} %collective-permute-done.4.recv_ref, f32[16,1408]{1,0:T(8,128)S(1)} %dynamic-slice_add_fusion.after_ref), custom_call_target="tpu_custom_call" | custom-call | flops 2000000000 | bytes 7000000 | tf_op jit(solution)/shard_map/place/pallas_call | solution.py:376
  21.9 0.0 collective-permute-done.3
  21.9 1.3 %collective-permute-start.5 = (bf16[16,1408]{1,0:T(8,128)(2,1)S(1)}, bf16[16,1408]{1,0:T(8,128)(2,1)S(1)}, u32[]{:S(2)}, u32[]{:S(2)}) collective-permute-start(bf16[16,1408]{1,0:T(8,128)(2,1)S(1)} %get-tuple-element.50), channel_id=1, source_target_pairs={{0,4},{1,5},{2,6},{3,7},{4,0},{5,1},{6,2},{7,3},{8,12},{9,13},{10,... | collective-permute-start | bytes 135176 | tf_op jit(solution)/shard_map/ppermute | solution.py:393
  23.3 2.9 %backward_own_planes.1.acc_ref = f32[2,640,256]{2,1,0:T(8,128)S(1)} custom-call(s32[2,32]{1,0:T(2,128)S(1)} %bitcast.5, f32[16,1408]{1,0:T(8,128)S(1)} %get-tuple-element.51.after_ref, bf16[512,512]{1,0:T(8,128)(2,1)S(1)} %get-tuple-element.37.gplanes_ref, bf16[96,288]{1,0:T(8,128)(2,1)S(1)} %get-tuple-element.38.flipped_ref), custom_call_target="tpu_custom_call" | custom-call | flops 3000000000 | bytes 10500000 | tf_op jit(solution)/shard_map/backward_own_planes/pallas_call | solution.py:376
  26.2 0.0 collective-permute-done.5
  26.3 2.4 %collective-permute-start.6 = (bf16[16,1408]{1,0:T(8,128)(2,1)S(1)}, bf16[16,1408]{1,0:T(8,128)(2,1)S(1)}, u32[]{:S(2)}, u32[]{:S(2)}) collective-permute-start(bf16[16,1408]{1,0:T(8,128)(2,1)S(1)} %get-tuple-element.48), channel_id=1, source_target_pairs={{0,8},{1,9},{2,10},{3,11},{4,12},{5,13},{6,14},{7,15},{8,0},{9,1},... | collective-permute-start | bytes 135176 | tf_op jit(solution)/shard_map/ppermute | solution.py:393
  28.6 0.0 collective-permute-done.7.cross_ref
  28.6 1.8 %backward_rest.1 = bf16[2,32,4096]{2,1,0:T(8,128)(2,1)} custom-call(s32[2,32]{1,0:T(2,128)S(1)} %bitcast.6, bf16[2,4096]{1,0:T(2,128)(2,1)S(1)} %get-tuple-element.40.mask_ref, f32[16,1408]{1,0:T(8,128)S(1)} %get-tuple-element.49.after_ref, f32[2,640,256]{2,1,0:T(8,128)S(1)} %backward_own_planes.1.acc_ref, ...), custom_call_target="tpu_custom_call" | custom-call | flops 2000000000 | bytes 7000000 | tf_op jit(solution)/shard_map/backward_rest/pallas_call | solution.py:376
  30.4 0.1 collective-permute-done.6
  30.5 2.3 %collective-permute-start.8 = (f32[16,1408]{1,0:T(8,128)S(1)}, f32[16,1408]{1,0:T(8,128)S(1)}, u32[]{:S(2)}, u32[]{:S(2)}) collective-permute-start(f32[16,1408]{1,0:T(8,128)S(1)} %reduce-precision_add_fusion.total_ref), channel_id=1, source_target_pairs={{0,1},{1,0},{2,3},{3,2},{4,5},{5,4},{6,7},{7,6},{8,9},{9,8},{10,11... | collective-permute-start | bytes 270344 | tf_op jit(solution)/shard_map/ppermute | solution.py:393
  32.8 0.9 %collective-permute-done.8.other_ref = f32[16,1408]{1,0:T(8,128)S(1)} collective-permute-done((f32[16,1408]{1,0:T(8,128)S(1)}, f32[16,1408]{1,0:T(8,128)S(1)}, u32[]{:S(2)}, u32[]{:S(2)}) %collective-permute-start.8) | collective-permute-done | bytes 90144 | tf_op jit(solution)/shard_map/ppermute | solution.py:393
  33.7 0.7 %finish.1 = (f32[32,864]{1,0:T(8,128)}, f32[64,256]{1,0:T(8,128)}) custom-call(f32[16,1408]{1,0:T(8,128)S(1)} %reduce-precision_add_fusion.total_ref, f32[16,1408]{1,0:T(8,128)S(1)} %collective-permute-done.8.other_ref), custom_call_target="tpu_custom_call" | custom-call | flops 1000000000 | bytes 3500000 | tf_op jit(solution)/shard_map/finish/pallas_call | solution.py:376
  (7 shorter events, 0.1 us)
Async XLA Ops:
  0.6 5.7 %copy-start.3 = (s32[32,2]{0,1:T(2,128)S(1)}, s32[32,2]{0,1:T(2,128)}, u32[]{:S(2)}) copy-start(s32[32,2]{0,1:T(2,128)} %param.9) | copy-start | bytes 772
  0.6 5.7 %copy-start = (bf16[2,32,4096]{2,1,0:T(8,128)(2,1)S(1)}, bf16[2,32,4096]{2,1,0:T(8,128)(2,1)}, u32[]{:S(2)}) copy-start(bf16[2,32,4096]{2,1,0:T(8,128)(2,1)} %feat_ref.1) | copy-start | bytes 1572868
  0.7 5.7 %copy-start.1 = (s32[2,4096]{1,0:T(2,128)S(1)}, s32[2,4096]{1,0:T(2,128)}, u32[]{:S(2)}) copy-start(s32[2,4096]{1,0:T(2,128)} %mask_hbm.3) | copy-start | bytes 98308
  3.6 7.1 %collective-permute-start = (bf16[96,1024]{1,0:T(8,128)(2,1)S(1)}, bf16[96,1024]{1,0:T(8,128)(2,1)S(1)}, u32[]{:S(2)}, u32[]{:S(2)}) collective-permute-start(bf16[96,1024]{1,0:T(8,128)(2,1)S(1)} %get-tuple-element.29), channel_id=1, source_target_pairs={{0,1},{1,0},{2,3},{3,2},{4,5},{5,4},{6,7},{7,6},{8,9},{9,8},{10,11... | collective-permute-start | bytes 589832 | tf_op jit(solution)/shard_map/ppermute | solution.py:393
  3.7 6.9 %collective-permute-start.1 = (bf16[32,512]{1,0:T(8,128)(2,1)S(1)}, bf16[32,512]{1,0:T(8,128)(2,1)S(1)}, u32[]{:S(2)}, u32[]{:S(2)}) collective-permute-start(bf16[32,512]{1,0:T(8,128)(2,1)S(1)} %get-tuple-element.30), channel_id=1, source_target_pairs={{0,16},{1,2},{2,1},{3,4},{4,3},{5,6},{6,5},{7,8},{8,7},{9,10},{10,... | collective-permute-start | bytes 98312 | tf_op jit(solution)/shard_map/ppermute | solution.py:407
  6.3 4.3 %copy-start.2 = (bf16[64,256]{1,0:T(8,128)(2,1)S(1)}, bf16[64,256]{1,0:T(8,128)(2,1)}, u32[]{:S(2)}) copy-start(bf16[64,256]{1,0:T(8,128)(2,1)} %down_hbm.3) | copy-start | bytes 98308
  16.6 1.4 %collective-permute-start.2 = (f32[16,1408]{1,0:T(8,128)S(1)}, f32[16,1408]{1,0:T(8,128)S(1)}, u32[]{:S(2)}, u32[]{:S(2)}) collective-permute-start(f32[16,1408]{1,0:T(8,128)S(1)} %constant_dynamic-slice_fusion), channel_id=1, source_target_pairs={{0,1},{1,0},{2,3},{3,2},{4,5},{5,4},{6,7},{7,6},{8,9},{9,8},{10,11... | collective-permute-start | bytes 270344 | tf_op jit(solution)/shard_map/ppermute | solution.py:393
  17.0 3.0 %collective-permute-start.4 = (bf16[96,1024]{1,0:T(8,128)(2,1)S(1)}, bf16[96,1024]{1,0:T(8,128)(2,1)S(1)}, u32[]{:S(2)}, u32[]{:S(2)}) collective-permute-start(bf16[96,1024]{1,0:T(8,128)(2,1)S(1)} %get-tuple-element.34.own_ref), channel_id=1, source_target_pairs={{0,1},{1,0},{2,3},{3,2},{4,5},{5,4},{6,7},{7,6},{8,9},{9,8},{10,11... | collective-permute-start | bytes 589832 | tf_op jit(solution)/shard_map/ppermute | solution.py:393
  18.0 3.9 %collective-permute-start.3 = (f32[16,1408]{1,0:T(8,128)S(1)}, f32[16,1408]{1,0:T(8,128)S(1)}, u32[]{:S(2)}, u32[]{:S(2)}) collective-permute-start(f32[16,1408]{1,0:T(8,128)S(1)} %dynamic-slice_add_fusion.after_ref), channel_id=1, source_target_pairs={{0,2},{1,3},{2,0},{3,1},{4,6},{5,7},{6,4},{7,5},{8,10},{9,11},{10,... | collective-permute-start | bytes 270344 | tf_op jit(solution)/shard_map/ppermute | solution.py:393
  19.3 9.4 %collective-permute-start.7 = (bf16[32,512]{1,0:T(8,128)(2,1)S(1)}, bf16[32,512]{1,0:T(8,128)(2,1)S(1)}, u32[]{:S(2)}, u32[]{:S(2)}) collective-permute-start(bf16[32,512]{1,0:T(8,128)(2,1)S(1)} %get-tuple-element.43), channel_id=1, source_target_pairs={{0,16},{1,2},{2,1},{3,4},{4,3},{5,6},{6,5},{7,8},{8,7},{9,10},{10,... | collective-permute-start | bytes 98312 | tf_op jit(solution)/shard_map/ppermute | solution.py:407
  21.9 4.3 %collective-permute-start.5 = (bf16[16,1408]{1,0:T(8,128)(2,1)S(1)}, bf16[16,1408]{1,0:T(8,128)(2,1)S(1)}, u32[]{:S(2)}, u32[]{:S(2)}) collective-permute-start(bf16[16,1408]{1,0:T(8,128)(2,1)S(1)} %get-tuple-element.50), channel_id=1, source_target_pairs={{0,4},{1,5},{2,6},{3,7},{4,0},{5,1},{6,2},{7,3},{8,12},{9,13},{10,... | collective-permute-start | bytes 135176 | tf_op jit(solution)/shard_map/ppermute | solution.py:393
  26.3 4.3 %collective-permute-start.6 = (bf16[16,1408]{1,0:T(8,128)(2,1)S(1)}, bf16[16,1408]{1,0:T(8,128)(2,1)S(1)}, u32[]{:S(2)}, u32[]{:S(2)}) collective-permute-start(bf16[16,1408]{1,0:T(8,128)(2,1)S(1)} %get-tuple-element.48), channel_id=1, source_target_pairs={{0,8},{1,9},{2,10},{3,11},{4,12},{5,13},{6,14},{7,15},{8,0},{9,1},... | collective-permute-start | bytes 135176 | tf_op jit(solution)/shard_map/ppermute | solution.py:393
  30.5 3.2 %collective-permute-start.8 = (f32[16,1408]{1,0:T(8,128)S(1)}, f32[16,1408]{1,0:T(8,128)S(1)}, u32[]{:S(2)}, u32[]{:S(2)}) collective-permute-start(f32[16,1408]{1,0:T(8,128)S(1)} %reduce-precision_add_fusion.total_ref), channel_id=1, source_target_pairs={{0,1},{1,0},{2,3},{3,2},{4,5},{5,4},{6,7},{7,6},{8,9},{9,8},{10,11... | collective-permute-start | bytes 270344 | tf_op jit(solution)/shard_map/ppermute | solution.py:393

commit v4 on v3

--- a/solution.py
+++ b/solution.py
@@ -75,7 +75,7 @@
     pairs += [(halves[0], grad_ref.at[0]), (halves[1], grad_ref.at[1])]
     copies = start_all(pairs, sems)
     row = iota((2 * PLANE, 2 * QUARTER), 0)
-    lane = iota((2 * PLANE, 2 * QUARTER), 1)
+    lane = iota((1, 2 * QUARTER), 1)
     picks = [one_hot(row, octant_key(xy_ref, target, parity, lane)) for target in (partner, layer)]
     for copy in copies[:2]:
         copy.wait()
@@ -176,7 +176,7 @@
 
 
 def inner_kernel(
-    xy_ref, feat_ref, mask_ref, stacked_ref, cols_hbm, acc_hbm, rows_ref, window_ref, in_ref, cols_ref, acc_ref, sems,
+    xy_ref, feat_ref, mask_ref, stacked_ref, cols_hbm, acc_ref, rows_ref, window_ref, in_ref, cols_ref, sems,
 ):
     layer = lax.axis_index("morton")
     build_masks(0, 0, rows_ref, window_ref.at[2])
@@ -195,10 +195,9 @@
         for i in range(2):
             unfold_planes(in_ref, r, i * STEP, ox[r], window_ref.at[2], window_ref.at[r], cols_ref.at[r])
             rows = pl.ds(i * STEP * 288, STEP * 288)
-            out += start_all(((cols_ref.at[r, rows], cols_hbm.at[r, rows]),), sems.at[pl.ds(2 + 2 * r + i, 1)])
+            out += start_all(((cols_ref.at[r, rows], cols_hbm.at[r, rows]),), sems.at[pl.ds(2 * r + i, 1)])
     for r in range(2):
         convolve(stacked_ref[...], cols_ref.at[r], acc_ref.at[r])
-        out += start_all(((acc_ref.at[r, pl.ds(64, 512)], acc_hbm.at[r, pl.ds(0, 512)]),), sems.at[pl.ds(r, 1)])
     for copy in out:
         copy.wait()
 
@@ -215,12 +214,12 @@
 
 
 def outer_kernel(
-    layers, scale, xy_ref, cols_hbm, acc_hbm, mask_hbm, down_hbm, recv_ref, cross_ref, own_ref, stacked_ref, down_t_ref,
+    layers, scale, xy_ref, cols_hbm, acc_ref, mask_hbm, down_hbm, recv_ref, cross_ref, own_ref, stacked_ref, down_t_ref,
     message_ref, gplanes_ref, gcross_ref, small_ref, sums_ref,
-    cols_ref, acc_ref, mask_ref, down_ref, gather_ref, act_ref, up_ref, stride_ref, grad_ref, total_ref, sems,
+    cols_ref, side_ref, mask_ref, down_ref, gather_ref, act_ref, up_ref, stride_ref, grad_ref, total_ref, sems,
 ):
     copies = start_all(
-        ((acc_hbm.at[:, pl.ds(0, 512)], acc_ref), (mask_hbm, mask_ref), (down_hbm, down_ref), (cols_hbm, cols_ref)), sems
+        ((mask_hbm, mask_ref), (down_hbm, down_ref), (cols_hbm, cols_ref)), sems
     )
     layer = lax.axis_index("morton")
     sides = sides_of(layer)
@@ -254,12 +253,12 @@
     for (other, dz, z), ref in zip(sides, (core_ref, cross_ref)):
         for r in range(2):
             side_cols.append(unfold_side(xy_ref, layers, layer, r, other, ref[...]))
-    for copy in copies[:3]:
+    for copy in copies[:2]:
         copy.wait()
     small_ref[...] = mask_ref[...].astype(F32).astype(BF16)
     for side, (other, dz, z) in enumerate(sides):
         for r in range(2):
-            acc_ref[r, rows_at(15 - z), :] += mm(stacked_ref[rows_at(dz), :], side_cols[side * 2 + r])
+            side_ref[r, dz // 2] = mm(stacked_ref[rows_at(dz), :], side_cols[side * 2 + r])
     zeros = jnp.zeros((64, PLANE), BF16)
     for r in range(2):
         grad_ref[r, pl.ds(0, 64), :] = zeros
@@ -269,7 +268,9 @@
             for kz in range(2):
                 z = 2 * wz + kz
                 mask = mask_ref[pl.ds(r, 1), pl.ds(z * PLANE, PLANE)].astype(F32)
-                pre = acc_ref[r, pl.ds((15 - z) * 32, 32), :]
+                pre = acc_ref[r, pl.ds((17 - z) * 32, 32), :]
+                if z in (0, EDGE - 1):
+                    pre = pre + side_ref[r, z // (EDGE - 1)]
                 sig = 1.0 / (1.0 + jnp.exp(-pre))
                 masked = sig * mask
                 act_ref[pl.ds(z * 32, 32), pl.ds(r * PLANE, PLANE)] = (pre * masked).astype(BF16)
@@ -291,7 +292,7 @@
     sums_ref[:, pl.ds(896, 256)] = down_sum[:32]
     sums_ref[:, pl.ds(1152, 256)] = down_sum[32:]
 
-    copies[3].wait()
+    copies[2].wait()
     total = jnp.zeros((288, 96), F32)
     for r in range(2):
         for p in range(EDGE):
@@ -436,23 +437,23 @@
     mask_rows = pltpu.VMEM((16, PLANE), F32)
     all_cols, acc = call(
         inner_kernel, "forward_own_planes",
-        [shape((2, 16 * 288, PLANE)), shape((2, 4096, PLANE), F32)],
-        (xy, features, voxel_mask, stacked), "svvv", out_kinds="hh",
+        [shape((2, 16 * 288, PLANE)), shape((2, 20 * 32, PLANE), F32)],
+        (xy, features, voxel_mask, stacked), "svvv", out_kinds="hv",
         scratch=[
             mask_rows, windows,
             pltpu.VMEM((512, 512), BF16),
-            two_cols, pltpu.VMEM((2, 20 * 32, PLANE), F32), pltpu.SemaphoreType.DMA((6,)),
+            two_cols, pltpu.SemaphoreType.DMA((4,)),
         ],
         us=5, vmem_mib=50,
     )
     message, gplanes, gcross, small_mask, sums = call(
         functools.partial(outer_kernel, layers, scale), "forward_rest",
         [message_shape, shape((512, 512)), side_shape, shape((2, voxels)), shape((32, 1408), F32)],
-        (xy, all_cols, acc, voxel_mask, down_weight, arrived, cross_side, own, stacked, down_t), "shhhhvvvvv",
+        (xy, all_cols, acc, voxel_mask, down_weight, arrived, cross_side, own, stacked, down_t), "shvhhvvvvv",
         scratch=[
-            two_cols, pltpu.VMEM((2, 512, PLANE), F32), mask, pltpu.VMEM((64, 256), BF16),
+            two_cols, pltpu.VMEM((2, 2, 32, PLANE), F32), mask, pltpu.VMEM((64, 256), BF16),
             pltpu.VMEM((2, 512, PLANE), BF16), pltpu.VMEM((512, 512), BF16), pltpu.VMEM((2, HALF, 256, PLANE), BF16), pltpu.VMEM((256, 1024), BF16),
-            pltpu.VMEM((2, 20 * 32, PLANE), BF16), pltpu.VMEM((96, 288), F32), pltpu.SemaphoreType.DMA((4,)),
+            pltpu.VMEM((2, 20 * 32, PLANE), BF16), pltpu.VMEM((96, 288), F32), pltpu.SemaphoreType.DMA((3,)),
         ],
         us=6, vmem_mib=50,
     )
@@ -462,7 +463,7 @@
     total = keep + exchange(lax.dynamic_slice_in_dim(sums, (1 - odd) * rows, rows, 0), 0)
     message_there = exchange(message, 0)
     for bit in range(1, rounds):
-        if bit < 2:
+        if bit < 3:
             sent = total
             step = exchange(sent, bit)
         else:

time: 34.9 us -> 34.5 us (0.989)
  Pallas kernels: 20.3 us -> 19.9 us
    pallas_call x7, Pallas kernels: 20.3 us -> 19.9 us  [call(): pl.pallas_call(body, name=name, out_shape=out_shapes, in_specs=[specs[kin...]
where the time goes in v4:
time: 34.5 us; the launch traced here: 34 us
  Pallas kernels  19.9 us (58%)
  starting transfers between devices  11.3 us (33%)
  waiting for transfers between devices  1.88 us (5%)
  between operations  0.81 us (2%)
    pallas_call x7, Pallas kernels, call(): pl.pallas_call(body, name=name, out_shape=out_shapes, in_specs=[specs[kin...  19.9 us
    ppermute x7, starting transfers between devices, exchange(): lax.ppermute(value, 'morton', [(i, i ^ 1 << bit) for i in range(lax.axis_...  7.93 us
    ppermute x2, starting transfers between devices, exchange_cross(): return lax.ppermute(value, ('groups', 'morton'), pairs)  3.41 us
    ppermute x7, waiting for transfers between devices, exchange(): lax.ppermute(value, 'morton', [(i, i ^ 1 << bit) for i in range(lax.axis_...  1.87 us
  transfers between devices with their start and end apart: 9, of which 3 were waited for; matrix products, arithmetic and copies ran while one was open for 0% of the time, Pallas kernels for 31%

profile of v4, /device:TPU:1, one launch (start us, length us, event | category | flops | bytes accessed | tf_op | source)
XLA Modules:
  0.0 34.0 jit_solution(5791914506753924982)
XLA Ops:
  0.6 0.0 copy-start
  0.6 0.0 copy-start.1
  0.7 0.0 copy-start.3
  0.7 2.9 %prepare.1 = (bf16[96,1024]{1,0:T(8,128)(2,1)S(1)}, bf16[32,512]{1,0:T(8,128)(2,1)S(1)}, bf16[64,1024]{1,0:T(8,128)(2,1)S(1)}, bf16[96,288]{1,0:T(8,128)(2,1)S(1...) custom-call(s32[2,32]{1,0:T(2,128)} %bitcast.1, bf16[2,32,4096]{2,1,0:T(8,128)(2,1)} %feat_ref.1, ...), custom_call_target="tpu_custom_call" | custom-call | flops 2000000000 | bytes 7000000 | tf_op jit(solution)/shard_map/prepare/pallas_call | solution.py:377
  3.6 0.1 collective-permute-start
  3.7 2.6 %collective-permute-start.1 = (bf16[32,512]{1,0:T(8,128)(2,1)S(1)}, bf16[32,512]{1,0:T(8,128)(2,1)S(1)}, u32[]{:S(2)}, u32[]{:S(2)}) collective-permute-start(bf16[32,512]{1,0:T(8,128)(2,1)S(1)} %get-tuple-element.30), channel_id=1, source_target_pairs={{0,16},{1,2},{2,1},{3,4},{4,3},{5,6},{6,5},{7,8},{8,7},{9,10},{10,... | collective-permute-start | bytes 98312 | tf_op jit(solution)/shard_map/ppermute | solution.py:408
  6.3 0.0 copy-done
  6.3 0.0 copy-done.1
  6.3 0.0 copy-done.3
  6.3 0.0 copy-start.2
  6.4 3.9 %forward_own_planes.1 = (bf16[2,4608,256]{2,1,0:T(8,128)(2,1)}, f32[2,640,256]{2,1,0:T(8,128)S(1)}) custom-call(s32[2,32]{1,0:T(2,128)S(1)} %bitcast.2, bf16[2,32,4096]{2,1,0:T(8,128)(2,1)S(1)} %copy-done, s32[2,4096]{1,0:T(2,128)S(1)} %copy-done.1, bf16[96,288]{1,0:T(8,128)(2,1)S(1)} %get-tuple-element.26.stacked_ref), custom_call_target="tpu_custom_call" | custom-call | flops 5000000000 | bytes 17500000 | tf_op jit(solution)/shard_map/forward_own_planes/pallas_call | solution.py:377
  10.3 0.0 collective-permute-done.1.cross_ref
  10.3 0.0 collective-permute-done.recv_ref
  10.3 0.0 copy-done.2
  10.3 5.8 %forward_rest.1 = (bf16[96,1024]{1,0:T(8,128)(2,1)S(1)}, bf16[512,512]{1,0:T(8,128)(2,1)S(1)}, bf16[32,512]{1,0:T(8,128)(2,1)S(1)}, bf16[2,4096]{1,0:T(2,128)(2,1)S(1)}, f32[32,1408]{1,0:T(8,128)S(1)}) custom-call(s32[2,32]{1,0:T(2,128)S(1)} %bitcast.3, bf16[2,4608,256]{2,1,0:T(8,128)(2,1)} %get-tuple-element.27.cols_hbm, ...), custom_call_target="tpu_custom_call" | custom-call | flops 6000000000 | bytes 21000000 | tf_op jit(solution)/shard_map/forward_rest/pallas_call | solution.py:377
  16.1 0.4 %collective-permute-start.2 = (f32[16,1408]{1,0:T(8,128)S(1)}, f32[16,1408]{1,0:T(8,128)S(1)}, u32[]{:S(2)}, u32[]{:S(2)}) collective-permute-start(f32[16,1408]{1,0:T(8,128)S(1)} %constant_dynamic-slice_fusion), channel_id=1, source_target_pairs={{0,1},{1,0},{2,3},{3,2},{4,5},{5,4},{6,7},{7,6},{8,9},{9,8},{10,11... | collective-permute-start | bytes 270344 | tf_op jit(solution)/shard_map/ppermute | solution.py:394
  16.6 0.1 collective-permute-start.4
  16.7 0.8 %collective-permute-done.2 = f32[16,1408]{1,0:T(8,128)S(1)} collective-permute-done((f32[16,1408]{1,0:T(8,128)S(1)}, f32[16,1408]{1,0:T(8,128)S(1)}, u32[]{:S(2)}, u32[]{:S(2)}) %collective-permute-start.2) | collective-permute-done | bytes 90144 | tf_op jit(solution)/shard_map/ppermute | solution.py:394
  17.5 1.3 %collective-permute-start.3 = (f32[16,1408]{1,0:T(8,128)S(1)}, f32[16,1408]{1,0:T(8,128)S(1)}, u32[]{:S(2)}, u32[]{:S(2)}) collective-permute-start(f32[16,1408]{1,0:T(8,128)S(1)} %dynamic-slice_add_fusion.after_ref), channel_id=1, source_target_pairs={{0,2},{1,3},{2,0},{3,1},{4,6},{5,7},{6,4},{7,5},{8,10},{9,11},{10,... | collective-permute-start | bytes 270344 | tf_op jit(solution)/shard_map/ppermute | solution.py:394
  18.8 0.8 %collective-permute-start.7 = (bf16[32,512]{1,0:T(8,128)(2,1)S(1)}, bf16[32,512]{1,0:T(8,128)(2,1)S(1)}, u32[]{:S(2)}, u32[]{:S(2)}) collective-permute-start(bf16[32,512]{1,0:T(8,128)(2,1)S(1)} %get-tuple-element.43), channel_id=1, source_target_pairs={{0,16},{1,2},{2,1},{3,4},{4,3},{5,6},{6,5},{7,8},{8,7},{9,10},{10,... | collective-permute-start | bytes 98312 | tf_op jit(solution)/shard_map/ppermute | solution.py:408
  19.6 0.0 collective-permute-done.4.recv_ref
  19.6 1.9 %place.1 = bf16[2,64,4096]{2,1,0:T(8,128)(2,1)} custom-call(s32[2,32]{1,0:T(2,128)S(1)} %bitcast.4, bf16[96,1024]{1,0:T(8,128)(2,1)S(1)} %get-tuple-element.34.own_ref, bf16[96,1024]{1,0:T(8,128)(2,1)S(1)} %collective-permute-done.4.recv_ref, f32[16,1408]{1,0:T(8,128)S(1)} %dynamic-slice_add_fusion.after_ref), custom_call_target="tpu_custom_call" | custom-call | flops 2000000000 | bytes 7000000 | tf_op jit(solution)/shard_map/place/pallas_call | solution.py:377
  21.5 0.0 collective-permute-done.3
  21.5 1.3 %collective-permute-start.5 = (f32[16,1408]{1,0:T(8,128)S(1)}, f32[16,1408]{1,0:T(8,128)S(1)}, u32[]{:S(2)}, u32[]{:S(2)}) collective-permute-start(f32[16,1408]{1,0:T(8,128)S(1)} %add.26.after_ref), channel_id=1, source_target_pairs={{0,4},{1,5},{2,6},{3,7},{4,0},{5,1},{6,2},{7,3},{8,12},{9,13},{10,... | collective-permute-start | bytes 270344 | tf_op jit(solution)/shard_map/ppermute | solution.py:394
  22.8 2.9 %backward_own_planes.1.acc_ref = f32[2,640,256]{2,1,0:T(8,128)S(1)} custom-call(s32[2,32]{1,0:T(2,128)S(1)} %bitcast.5, f32[16,1408]{1,0:T(8,128)S(1)} %add.26.after_ref, bf16[512,512]{1,0:T(8,128)(2,1)S(1)} %get-tuple-element.37.gplanes_ref, bf16[96,288]{1,0:T(8,128)(2,1)S(1)} %get-tuple-element.38.flipped_ref), custom_call_target="tpu_custom_call" | custom-call | flops 3000000000 | bytes 10500000 | tf_op jit(solution)/shard_map/backward_own_planes/pallas_call | solution.py:377
  25.8 0.0 collective-permute-done.5
  25.8 2.4 %collective-permute-start.6 = (bf16[16,1408]{1,0:T(8,128)(2,1)S(1)}, bf16[16,1408]{1,0:T(8,128)(2,1)S(1)}, u32[]{:S(2)}, u32[]{:S(2)}) collective-permute-start(bf16[16,1408]{1,0:T(8,128)(2,1)S(1)} %get-tuple-element.48), channel_id=1, source_target_pairs={{0,8},{1,9},{2,10},{3,11},{4,12},{5,13},{6,14},{7,15},{8,0},{9,1},... | collective-permute-start | bytes 135176 | tf_op jit(solution)/shard_map/ppermute | solution.py:394
  28.2 0.0 collective-permute-done.7.cross_ref
  28.2 1.8 %backward_rest.1 = bf16[2,32,4096]{2,1,0:T(8,128)(2,1)} custom-call(s32[2,32]{1,0:T(2,128)S(1)} %bitcast.6, bf16[2,4096]{1,0:T(2,128)(2,1)S(1)} %get-tuple-element.40.mask_ref, f32[16,1408]{1,0:T(8,128)S(1)} %get-tuple-element.49.after_ref, f32[2,640,256]{2,1,0:T(8,128)S(1)} %backward_own_planes.1.acc_ref, ...), custom_call_target="tpu_custom_call" | custom-call | flops 2000000000 | bytes 7000000 | tf_op jit(solution)/shard_map/backward_rest/pallas_call | solution.py:377
  30.0 0.1 collective-permute-done.6
  30.2 2.2 %collective-permute-start.8 = (f32[16,1408]{1,0:T(8,128)S(1)}, f32[16,1408]{1,0:T(8,128)S(1)}, u32[]{:S(2)}, u32[]{:S(2)}) collective-permute-start(f32[16,1408]{1,0:T(8,128)S(1)} %reduce-precision_add_fusion.total_ref), channel_id=1, source_target_pairs={{0,1},{1,0},{2,3},{3,2},{4,5},{5,4},{6,7},{7,6},{8,9},{9,8},{10,11... | collective-permute-start | bytes 270344 | tf_op jit(solution)/shard_map/ppermute | solution.py:394
  32.4 0.9 %collective-permute-done.8.other_ref = f32[16,1408]{1,0:T(8,128)S(1)} collective-permute-done((f32[16,1408]{1,0:T(8,128)S(1)}, f32[16,1408]{1,0:T(8,128)S(1)}, u32[]{:S(2)}, u32[]{:S(2)}) %collective-permute-start.8) | collective-permute-done | bytes 90144 | tf_op jit(solution)/shard_map/ppermute | solution.py:394
  33.3 0.7 %finish.1 = (f32[32,864]{1,0:T(8,128)}, f32[64,256]{1,0:T(8,128)}) custom-call(f32[16,1408]{1,0:T(8,128)S(1)} %reduce-precision_add_fusion.total_ref, f32[16,1408]{1,0:T(8,128)S(1)} %collective-permute-done.8.other_ref), custom_call_target="tpu_custom_call" | custom-call | flops 1000000000 | bytes 3500000 | tf_op jit(solution)/shard_map/finish/pallas_call | solution.py:377
  (6 shorter events, 0.1 us)
Async XLA Ops:
  0.6 5.7 %copy-start = (bf16[2,32,4096]{2,1,0:T(8,128)(2,1)S(1)}, bf16[2,32,4096]{2,1,0:T(8,128)(2,1)}, u32[]{:S(2)}) copy-start(bf16[2,32,4096]{2,1,0:T(8,128)(2,1)} %feat_ref.1) | copy-start | bytes 1572868
  0.6 5.7 %copy-start.1 = (s32[2,4096]{1,0:T(2,128)S(1)}, s32[2,4096]{1,0:T(2,128)}, u32[]{:S(2)}) copy-start(s32[2,4096]{1,0:T(2,128)} %mask_hbm.3) | copy-start | bytes 98308
  0.7 5.7 %copy-start.3 = (s32[32,2]{0,1:T(2,128)S(1)}, s32[32,2]{0,1:T(2,128)}, u32[]{:S(2)}) copy-start(s32[32,2]{0,1:T(2,128)} %param.9) | copy-start | bytes 772
  3.6 6.7 %collective-permute-start = (bf16[96,1024]{1,0:T(8,128)(2,1)S(1)}, bf16[96,1024]{1,0:T(8,128)(2,1)S(1)}, u32[]{:S(2)}, u32[]{:S(2)}) collective-permute-start(bf16[96,1024]{1,0:T(8,128)(2,1)S(1)} %get-tuple-element.29), channel_id=1, source_target_pairs={{0,1},{1,0},{2,3},{3,2},{4,5},{5,4},{6,7},{7,6},{8,9},{9,8},{10,11... | collective-permute-start | bytes 589832 | tf_op jit(solution)/shard_map/ppermute | solution.py:394
  3.7 6.6 %collective-permute-start.1 = (bf16[32,512]{1,0:T(8,128)(2,1)S(1)}, bf16[32,512]{1,0:T(8,128)(2,1)S(1)}, u32[]{:S(2)}, u32[]{:S(2)}) collective-permute-start(bf16[32,512]{1,0:T(8,128)(2,1)S(1)} %get-tuple-element.30), channel_id=1, source_target_pairs={{0,16},{1,2},{2,1},{3,4},{4,3},{5,6},{6,5},{7,8},{8,7},{9,10},{10,... | collective-permute-start | bytes 98312 | tf_op jit(solution)/shard_map/ppermute | solution.py:408
  6.3 4.0 %copy-start.2 = (bf16[64,256]{1,0:T(8,128)(2,1)S(1)}, bf16[64,256]{1,0:T(8,128)(2,1)}, u32[]{:S(2)}) copy-start(bf16[64,256]{1,0:T(8,128)(2,1)} %down_hbm.3) | copy-start | bytes 98308
  16.1 1.4 %collective-permute-start.2 = (f32[16,1408]{1,0:T(8,128)S(1)}, f32[16,1408]{1,0:T(8,128)S(1)}, u32[]{:S(2)}, u32[]{:S(2)}) collective-permute-start(f32[16,1408]{1,0:T(8,128)S(1)} %constant_dynamic-slice_fusion), channel_id=1, source_target_pairs={{0,1},{1,0},{2,3},{3,2},{4,5},{5,4},{6,7},{7,6},{8,9},{9,8},{10,11... | collective-permute-start | bytes 270344 | tf_op jit(solution)/shard_map/ppermute | solution.py:394
  16.6 3.0 %collective-permute-start.4 = (bf16[96,1024]{1,0:T(8,128)(2,1)S(1)}, bf16[96,1024]{1,0:T(8,128)(2,1)S(1)}, u32[]{:S(2)}, u32[]{:S(2)}) collective-permute-start(bf16[96,1024]{1,0:T(8,128)(2,1)S(1)} %get-tuple-element.34.own_ref), channel_id=1, source_target_pairs={{0,1},{1,0},{2,3},{3,2},{4,5},{5,4},{6,7},{7,6},{8,9},{9,8},{10,11... | collective-permute-start | bytes 589832 | tf_op jit(solution)/shard_map/ppermute | solution.py:394
  17.5 3.9 %collective-permute-start.3 = (f32[16,1408]{1,0:T(8,128)S(1)}, f32[16,1408]{1,0:T(8,128)S(1)}, u32[]{:S(2)}, u32[]{:S(2)}) collective-permute-start(f32[16,1408]{1,0:T(8,128)S(1)} %dynamic-slice_add_fusion.after_ref), channel_id=1, source_target_pairs={{0,2},{1,3},{2,0},{3,1},{4,6},{5,7},{6,4},{7,5},{8,10},{9,11},{10,... | collective-permute-start | bytes 270344 | tf_op jit(solution)/shard_map/ppermute | solution.py:394
  18.8 9.4 %collective-permute-start.7 = (bf16[32,512]{1,0:T(8,128)(2,1)S(1)}, bf16[32,512]{1,0:T(8,128)(2,1)S(1)}, u32[]{:S(2)}, u32[]{:S(2)}) collective-permute-start(bf16[32,512]{1,0:T(8,128)(2,1)S(1)} %get-tuple-element.43), channel_id=1, source_target_pairs={{0,16},{1,2},{2,1},{3,4},{4,3},{5,6},{6,5},{7,8},{8,7},{9,10},{10,... | collective-permute-start | bytes 98312 | tf_op jit(solution)/shard_map/ppermute | solution.py:408
  21.5 4.3 %collective-permute-start.5 = (f32[16,1408]{1,0:T(8,128)S(1)}, f32[16,1408]{1,0:T(8,128)S(1)}, u32[]{:S(2)}, u32[]{:S(2)}) collective-permute-start(f32[16,1408]{1,0:T(8,128)S(1)} %add.26.after_ref), channel_id=1, source_target_pairs={{0,4},{1,5},{2,6},{3,7},{4,0},{5,1},{6,2},{7,3},{8,12},{9,13},{10,... | collective-permute-start | bytes 270344 | tf_op jit(solution)/shard_map/ppermute | solution.py:394
  25.8 4.3 %collective-permute-start.6 = (bf16[16,1408]{1,0:T(8,128)(2,1)S(1)}, bf16[16,1408]{1,0:T(8,128)(2,1)S(1)}, u32[]{:S(2)}, u32[]{:S(2)}) collective-permute-start(bf16[16,1408]{1,0:T(8,128)(2,1)S(1)} %get-tuple-element.48), channel_id=1, source_target_pairs={{0,8},{1,9},{2,10},{3,11},{4,12},{5,13},{6,14},{7,15},{8,0},{9,1},... | collective-permute-start | bytes 135176 | tf_op jit(solution)/shard_map/ppermute | solution.py:394
  30.2 3.1 %collective-permute-start.8 = (f32[16,1408]{1,0:T(8,128)S(1)}, f32[16,1408]{1,0:T(8,128)S(1)}, u32[]{:S(2)}, u32[]{:S(2)}) collective-permute-start(f32[16,1408]{1,0:T(8,128)S(1)} %reduce-precision_add_fusion.total_ref), channel_id=1, source_target_pairs={{0,1},{1,0},{2,3},{3,2},{4,5},{5,4},{6,7},{7,6},{8,9},{9,8},{10,11... | collective-permute-start | bytes 270344 | tf_op jit(solution)/shard_map/ppermute | solution.py:394
